TPU v7x, 32 devices: a whole 2x2x4 slice. The times are simulated.
32 devices in a mesh: dp: 4 (over y, x), row: 4 (over z), col: 2 (over core).
Axes of the slice: x: 2, y: 2, z: 4, core: 2. Of those that a mesh axis runs over, the one named last changes fastest.
Arguments:
- inputs: bfloat16 [2916, 1152], P('dp', ('row', 'col')), may hold values from -11 to 11
- cotangent: bfloat16 [2916, 1152], P('dp', ('row', 'col')), may hold values from -6 to 6
- qkv_master: float32 [288, 4, 3456], P('row', 'dp', 'col'), may hold values from -0.1875 to 0.1875
- out_master: float32 [1152, 288, 4], P('col', 'row', 'dp'), may hold values from -1 to 1
- up_master: float32 [288, 4, 4304], P('row', 'dp', 'col'), may hold values from -0.20623948 to 0.20623948
- down_master: float32 [4304, 288, 4], P('col', 'row', 'dp'), may hold values from -0.09375 to 0.09375
- qkv_first: float32 [288, 4, 3456], P('row', 'dp', 'col'), may hold values from -16 to 16
- out_first: float32 [1152, 288, 4], P('col', 'row', 'dp'), may hold values from -6 to 6
- up_first: float32 [288, 4, 4304], P('row', 'dp', 'col'), may hold values from -6 to 6
- down_first: float32 [4304, 288, 4], P('col', 'row', 'dp'), may hold values from -20 to 20
- qkv_second: float32 [288, 4, 3456], P('row', 'dp', 'col'), may hold values from 0.729 to 2.916
- out_second: float32 [1152, 288, 4], P('col', 'row', 'dp'), may hold values from 0.06561 to 0.26244
- up_second: float32 [288, 4, 4304], P('row', 'dp', 'col'), may hold values from 0.26244 to 1.04976
- down_second: float32 [4304, 288, 4], P('col', 'row', 'dp'), may hold values from 1.04976 to 4.19904
- norm_gains: float32 [2, 1152], replicated, may hold values from 0.5 to 1.5
- gain_first: float32 [2, 1152], replicated, may hold values from -32 to 32
- gain_second: float32 [2, 1152], replicated, may hold values from 2.916 to 11.664
- biases: float32 [11216], replicated, may hold values from -1.5 to 1.5
- bias_first: float32 [11216], replicated, may hold values from -32 to 32
- bias_second: float32 [11216], replicated, may hold values from 2.916 to 11.664
Outputs:
- outputs: bfloat16 [2916, 1152], P('dp', ('row', 'col'))
- input_grad: bfloat16 [2916, 1152], P('dp', ('row', 'col'))
- new_qkv: float32 [288, 4, 3456], P('row', 'dp', 'col')
- new_qkv_first: float32 [288, 4, 3456], P('row', 'dp', 'col')
- new_qkv_second: float32 [288, 4, 3456], P('row', 'dp', 'col')
- new_out: float32 [1152, 288, 4], P('col', 'row', 'dp')
- new_out_first: float32 [1152, 288, 4], P('col', 'row', 'dp')
- new_out_second: float32 [1152, 288, 4], P('col', 'row', 'dp')
- new_up: float32 [288, 4, 4304], P('row', 'dp', 'col')
- new_up_first: float32 [288, 4, 4304], P('row', 'dp', 'col')
- new_up_second: float32 [288, 4, 4304], P('row', 'dp', 'col')
- new_down: float32 [4304, 288, 4], P('col', 'row', 'dp')
- new_down_first: float32 [4304, 288, 4], P('col', 'row', 'dp')
- new_down_second: float32 [4304, 288, 4], P('col', 'row', 'dp')
- new_gains: float32 [2, 1152], replicated
- new_gain_first: float32 [2, 1152], replicated
- new_gain_second: float32 [2, 1152], replicated
- new_biases: float32 [11216], replicated
- new_bias_first: float32 [11216], replicated
- new_bias_second: float32 [11216], replicated
All inputs are finite; a program needn't handle non-finite values.
Results may differ from a plain program's by a relative error of at most 0.02.
Values may be sent and summed in bfloat16 or wider, within the bound.
No kernel may reach another device: no remote copies, remote signals or barrier semaphores. Data moves between devices by JAX's collectives and lax.ppermute only.
A program may use at most 128 MiB of HBM per device.

v0:
```python
from functools import partial

import jax
import jax.numpy as jnp
from jax import lax
from jax.sharding import PartitionSpec as P

D = 1152
FF = 4304
HEAD = 72
SEQ = 729
STEP = 10


NORM_EPS = 1e-06
ADAM_EPS = 1e-08
BETA_ONE = 0.9
BETA_TWO = 0.999


def as_sent(value):
    return jax.tree.map(lambda a: a.astype(jnp.bfloat16) if a.dtype == jnp.float32 else a, value)


def contract(left_side, right_side, left_dim, right_dim):
    return lax.dot_general(
        left_side,
        right_side,
        (((left_dim,), (right_dim,)), ((), ())),
        preferred_element_type=jnp.float32,
    )


def segment_of(vector, offset, length):
    return lax.dynamic_slice_in_dim(vector, offset, length, axis=vector.ndim - 1)


def placed(vector, segment, offset):
    return lax.dynamic_update_slice_in_dim(vector, segment, offset, axis=vector.ndim - 1)


def widen(operand):
    return lax.all_gather(operand, "col", axis=1, tiled=True)


def spread_out(operand):
    return lax.all_gather(as_sent(operand), "row", axis=1, tiled=True).astype(operand.dtype)


def reduce_inner(term):
    return lax.psum_scatter(term, "row", scatter_dimension=1, tiled=True)


def reduce_outer(term):
    return lax.psum_scatter(
        term.astype(jnp.bfloat16), "col", scatter_dimension=1, tiled=True
    ).astype(jnp.float32)


def norm_forward(operand, norm_gain, norm_shift):
    average = lax.psum(jnp.sum(operand, axis=1), ("row", "col")) / D
    center = operand - average[:, None]
    spread = lax.psum(jnp.sum(center * center, axis=1), ("row", "col")) / D
    inverse = lax.rsqrt(spread + NORM_EPS)
    normed = center * inverse[:, None]
    return (normed * norm_gain + norm_shift, normed, inverse)


def norm_backward(out_grad, normed, inverse, norm_gain):
    scaled = out_grad * norm_gain
    first_sum, second_sum = lax.psum(
        (jnp.sum(scaled, axis=1), jnp.sum(scaled * normed, axis=1)), ("row", "col")
    )
    result = inverse[:, None] * (
        scaled - first_sum[:, None] / D - normed * (second_sum[:, None] / D)
    )
    return (result, jnp.sum(out_grad * normed, axis=0), jnp.sum(out_grad, axis=0))


def attend_forward(image_qkv):
    queries = image_qkv[:, :, 0]
    key_rows = image_qkv[:, :, 1]
    values = image_qkv[:, :, 2]
    scores = jnp.einsum(
        "qhe,khe->hqk", queries, key_rows, preferred_element_type=jnp.float32
    ) * HEAD ** (-0.5)
    row_max = jnp.max(scores, axis=2, keepdims=True)
    exponent = jnp.exp(scores - row_max)
    row_total = jnp.sum(exponent, axis=2, keepdims=True)
    probs_low = (exponent / row_total).astype(jnp.bfloat16)
    attended = jnp.einsum("hqk,khe->qhe", probs_low, values, preferred_element_type=jnp.float32)
    return (attended, row_max[:, :, 0] + jnp.log(row_total[:, :, 0]))


def attend_backward(operands):
    image_qkv, log_total, attended_grad = operands
    queries = image_qkv[:, :, 0]
    key_rows = image_qkv[:, :, 1]
    values = image_qkv[:, :, 2]
    scale = HEAD ** (-0.5)
    scores = (
        jnp.einsum("qhe,khe->hqk", queries, key_rows, preferred_element_type=jnp.float32) * scale
    )
    attn_probs = jnp.exp(scores - log_total[:, :, None])
    probs_low = attn_probs.astype(jnp.bfloat16)
    value_grad = jnp.einsum(
        "hqk,qhe->khe", probs_low, attended_grad, preferred_element_type=jnp.float32
    )
    probs_grad = jnp.einsum(
        "qhe,khe->hqk", attended_grad, values, preferred_element_type=jnp.float32
    )
    inner = jnp.sum(attn_probs * probs_grad, axis=2, keepdims=True)
    scores_grad = (attn_probs * (probs_grad - inner)).astype(jnp.bfloat16)
    query_grad = (
        jnp.einsum("hqk,khe->qhe", scores_grad, key_rows, preferred_element_type=jnp.float32)
        * scale
    )
    key_grad = (
        jnp.einsum("hqk,qhe->khe", scores_grad, queries, preferred_element_type=jnp.float32) * scale
    )
    return jnp.stack([query_grad, key_grad, value_grad], axis=2).astype(jnp.bfloat16)


def adam_update(weights, moment_one, second, gradient, step_rate, weight_decay):
    moment_one = BETA_ONE * moment_one + (1.0 - BETA_ONE) * gradient
    second = BETA_TWO * second + (1.0 - BETA_TWO) * gradient * gradient
    direction = (
        moment_one / (1.0 - BETA_ONE**STEP) / (jnp.sqrt(second / (1.0 - BETA_TWO**STEP)) + ADAM_EPS)
    )
    return (weights - step_rate * (direction + weight_decay * weights), moment_one, second)


def shards(
    inputs,
    cotangent,
    qkv_master,
    out_master,
    up_master,
    down_master,
    qkv_first,
    out_first,
    up_first,
    down_first,
    qkv_second,
    out_second,
    up_second,
    down_second,
    norm_gains,
    gain_first,
    gain_second,
    biases,
    bias_first,
    bias_second,
):
    tokens = inputs.shape[0]
    local_width = inputs.shape[1]
    n_row = lax.axis_size("row")
    n_col = lax.axis_size("col")
    n_images = lax.axis_size("dp")
    row_slot = lax.axis_index("row")
    col_slot = lax.axis_index("col")
    feature_slot = row_slot * n_col + col_slot
    head_slot = col_slot * n_row + row_slot
    local_heads = local_width // HEAD
    local_hidden = FF // (n_row * n_col)
    feature_start = feature_slot * local_width
    head_start = head_slot * local_width
    hidden_start = head_slot * local_hidden
    gain_one = segment_of(norm_gains[0], feature_start, local_width)
    gain_two = segment_of(norm_gains[1], feature_start, local_width)
    shift_one = segment_of(biases, feature_start, local_width)
    shift_two = segment_of(biases, D + feature_start, local_width)
    query_bias = segment_of(biases, 2 * D + head_start, local_width).reshape(local_heads, HEAD)
    value_bias = segment_of(biases, 3 * D + head_start, local_width).reshape(local_heads, HEAD)
    out_bias = segment_of(biases, 4 * D + feature_start, local_width)
    down_bias = segment_of(biases, 5 * D + feature_start, local_width)
    up_bias = segment_of(biases, 6 * D + hidden_start, local_hidden)
    qkv_bias = jnp.stack([query_bias, jnp.zeros_like(query_bias), value_bias], axis=1).reshape(
        3 * local_width
    )
    masters_low = (
        qkv_master.astype(jnp.bfloat16),
        out_master.astype(jnp.bfloat16),
        up_master.astype(jnp.bfloat16),
        down_master.astype(jnp.bfloat16),
    )
    qkv_rows, out_rows, up_rows, down_rows = (
        lax.all_gather(masters_low[0], "dp", axis=1, tiled=True),
        lax.all_gather(masters_low[1], "dp", axis=2, tiled=True),
        lax.all_gather(masters_low[2], "dp", axis=1, tiled=True),
        lax.all_gather(masters_low[3], "dp", axis=2, tiled=True),
    )
    w_qkv = qkv_rows.reshape(-1, qkv_rows.shape[2])
    w_out = out_rows.reshape(out_rows.shape[0], -1)
    w_up = up_rows.reshape(-1, up_rows.shape[2])
    w_down = down_rows.reshape(down_rows.shape[0], -1)
    inputs_full = inputs.astype(jnp.float32)
    z_one, normed_one, inverse_one = norm_forward(inputs_full, gain_one, shift_one)
    za_wide = widen(z_one.astype(jnp.bfloat16))
    qkv = (reduce_inner(contract(za_wide, w_qkv, 1, 0)) + qkv_bias).astype(jnp.bfloat16)
    qkv_images = qkv.reshape(tokens // SEQ, SEQ, local_heads, 3, HEAD)
    attended, log_total = lax.map(attend_forward, qkv_images)
    attended_wide = spread_out(attended.reshape(tokens, local_width).astype(jnp.bfloat16))
    middle = inputs_full + reduce_outer(contract(attended_wide, w_out, 1, 0)) + out_bias
    z_two, normed_two, inverse_two = norm_forward(middle, gain_two, shift_two)
    zb_wide = widen(z_two.astype(jnp.bfloat16))
    hidden = reduce_inner(contract(zb_wide, w_up, 1, 0)) + up_bias
    active, gelu_pullback = jax.vjp(partial(jax.nn.gelu, approximate=True), hidden)
    active_wide = spread_out(active.astype(jnp.bfloat16))
    result = (middle + reduce_outer(contract(active_wide, w_down, 1, 0)) + down_bias).astype(
        jnp.bfloat16
    )
    cot_wide = widen(cotangent)
    down_grad = contract(active_wide, cot_wide, 0, 0)
    down_bias_grad = jnp.sum(cotangent.astype(jnp.float32), axis=0)
    active_grad = reduce_inner(contract(cot_wide, w_down, 1, 1))
    hidden_grad = gelu_pullback(active_grad)[0].astype(jnp.bfloat16)
    up_bias_grad = jnp.sum(hidden_grad, axis=0, dtype=jnp.float32)
    hidden_wide = spread_out(hidden_grad)
    up_grad = contract(zb_wide, hidden_wide, 0, 0)
    two_grad = reduce_outer(contract(hidden_wide, w_up, 1, 1))
    norm_part, gain_two_grad, shift_two_grad = norm_backward(
        two_grad, normed_two, inverse_two, gain_two
    )
    middle_grad = cotangent.astype(jnp.float32) + norm_part
    branch_grad = middle_grad.astype(jnp.bfloat16)
    out_bias_grad = jnp.sum(branch_grad, axis=0, dtype=jnp.float32)
    branch_wide = widen(branch_grad)
    out_grad = contract(attended_wide, branch_wide, 0, 0)
    attended_grad = reduce_inner(contract(branch_wide, w_out, 1, 1)).astype(jnp.bfloat16)
    qkv_grad = lax.map(
        attend_backward,
        (qkv_images, log_total, attended_grad.reshape(tokens // SEQ, SEQ, local_heads, HEAD)),
    )
    qkv_grad = qkv_grad.reshape(tokens, 3 * local_width)
    bias_sums = jnp.sum(qkv_grad, axis=0, dtype=jnp.float32).reshape(local_heads, 3, HEAD)
    qkv_wide = spread_out(qkv_grad)
    qkv_weight_grad = contract(za_wide, qkv_wide, 0, 0)
    one_grad = reduce_outer(contract(qkv_wide, w_qkv, 1, 1))
    norm_first, gain_one_grad, shift_one_grad = norm_backward(
        one_grad, normed_one, inverse_one, gain_one
    )
    input_grad = (middle_grad + norm_first).astype(jnp.bfloat16)
    qkv_blocks = qkv_weight_grad.reshape(qkv_master.shape[0], n_images, -1)
    up_blocks = up_grad.reshape(up_master.shape[0], n_images, -1)
    out_blocks = out_grad.reshape(out_master.shape[0], out_master.shape[1], n_images)
    down_blocks = down_grad.reshape(down_master.shape[0], down_master.shape[1], n_images)
    reduced = (
        lax.psum_scatter(
            qkv_blocks.astype(jnp.bfloat16), "dp", scatter_dimension=1, tiled=True
        ).astype(jnp.float32),
        lax.psum_scatter(
            out_blocks.astype(jnp.bfloat16), "dp", scatter_dimension=2, tiled=True
        ).astype(jnp.float32),
        lax.psum_scatter(
            up_blocks.astype(jnp.bfloat16), "dp", scatter_dimension=1, tiled=True
        ).astype(jnp.float32),
        lax.psum_scatter(
            down_blocks.astype(jnp.bfloat16), "dp", scatter_dimension=2, tiled=True
        ).astype(jnp.float32),
    )
    gain_grad = placed(
        jnp.zeros(norm_gains.shape, jnp.float32),
        jnp.stack([gain_one_grad, gain_two_grad]),
        feature_start,
    )
    bias_grad = jnp.zeros(biases.shape, jnp.float32)
    bias_grad = placed(bias_grad, shift_one_grad, feature_start)
    bias_grad = placed(bias_grad, shift_two_grad, D + feature_start)
    bias_grad = placed(bias_grad, bias_sums[:, 0].reshape(local_width), 2 * D + head_start)
    bias_grad = placed(bias_grad, bias_sums[:, 2].reshape(local_width), 3 * D + head_start)
    bias_grad = placed(bias_grad, out_bias_grad, 4 * D + feature_start)
    bias_grad = placed(bias_grad, down_bias_grad, 5 * D + feature_start)
    bias_grad = placed(bias_grad, up_bias_grad, 6 * D + hidden_start)
    gain_total, bias_total = lax.psum((gain_grad, bias_grad), ("dp", "row", "col"))
    q_new, q_one, q_two = adam_update(qkv_master, qkv_first, qkv_second, reduced[0], 0.03, 0.1)
    o_new, o_one, o_two = adam_update(out_master, out_first, out_second, reduced[1], 0.12, 0.1)
    u_new, u_one, u_two = adam_update(up_master, up_first, up_second, reduced[2], 0.03, 0.1)
    d_new, d_one, d_two = adam_update(down_master, down_first, down_second, reduced[3], 0.02, 0.1)
    g_new, g_one, g_two = adam_update(norm_gains, gain_first, gain_second, gain_total, 0.5, 0.0)
    b_new, b_one, b_two = adam_update(biases, bias_first, bias_second, bias_total, 0.5, 0.0)
    return (
        result,
        input_grad,
        q_new,
        q_one,
        q_two,
        o_new,
        o_one,
        o_two,
        u_new,
        u_one,
        u_two,
        d_new,
        d_one,
        d_two,
        g_new,
        g_one,
        g_two,
        b_new,
        b_one,
        b_two,
    )


def solution(mesh):
    placed = (
        P("dp", ("row", "col")),
        P("dp", ("row", "col")),
        P("row", "dp", "col"),
        P("col", "row", "dp"),
        P("row", "dp", "col"),
        P("col", "row", "dp"),
        P("row", "dp", "col"),
        P("col", "row", "dp"),
        P("row", "dp", "col"),
        P("col", "row", "dp"),
        P("row", "dp", "col"),
        P("col", "row", "dp"),
        P("row", "dp", "col"),
        P("col", "row", "dp"),
        P(),
        P(),
        P(),
        P(),
        P(),
        P(),
    )
    return jax.shard_map(
        shards,
        mesh=mesh,
        in_specs=placed,
        out_specs=(
            P("dp", ("row", "col")),
            P("dp", ("row", "col")),
            P("row", "dp", "col"),
            P("row", "dp", "col"),
            P("row", "dp", "col"),
            P("col", "row", "dp"),
            P("col", "row", "dp"),
            P("col", "row", "dp"),
            P("row", "dp", "col"),
            P("row", "dp", "col"),
            P("row", "dp", "col"),
            P("col", "row", "dp"),
            P("col", "row", "dp"),
            P("col", "row", "dp"),
            P(),
            P(),
            P(),
            P(),
            P(),
            P(),
        ),
        check_vma=False,
    )
```

profile of v0, /device:TPU:0, one launch (start us, length us, event | category | flops | bytes accessed | tf_op | source)
XLA Modules:
  0.0 863.4 jit_solution(12188637099647983212)
XLA Ops:
  9.9 18.1 %psum.70 = f32[729]{0:T(1024)S(1)} all-reduce(f32[729]{0:T(1024)S(1)} %convert_reduce_fusion.4), channel_id=1, replica_groups=mesh['dp'=4,'row'=4,'col'=2] {'row','col'}, use_global_device_ids=true, to_apply=%region_1.0 | all-reduce | flops 729 | bytes 5832 | tf_op jit(solution)/shard_map/psum | solution.py:61
  29.0 13.6 %psum.71 = f32[729]{0:T(1024)S(1)} all-reduce(f32[729]{0:T(1024)S(1)} %fusion.45), channel_id=1, replica_groups=mesh['dp'=4,'row'=4,'col'=2] {'row','col'}, use_global_device_ids=true, to_apply=%region_3.0 | all-reduce | flops 729 | bytes 5832 | tf_op jit(solution)/shard_map/psum | solution.py:63
  48.6 14.2 %all_gather.37 = bf16[72,4,1728]{2,0,1:T(8,128)(2,1)S(1)} all-gather(bf16[72,1,1728]{2,0,1:T(8,128)(2,1)S(1)} %copy.188), channel_id=1, replica_groups=mesh['dp'=4,'row'=4,'col'=2] {'dp'}, dimensions={1}, use_global_device_ids=true | all-gather | bytes 1244160 | tf_op jit(solution)/shard_map/all_gather | solution.py:188
  63.6 3.9 fusion.79
  70.8 11.4 %all_gather.39 = bf16[576,72,4]{0,1,2:T(8,128)(2,1)S(1)} all-gather(bf16[576,72,1]{0,1,2:T(8,128)(2,1)S(1)} %copy.189), channel_id=1, replica_groups=mesh['dp'=4,'row'=4,'col'=2] {'dp'}, dimensions={2}, use_global_device_ids=true | all-gather | bytes 414720 | tf_op jit(solution)/shard_map/all_gather | solution.py:189
  82.5 77.3 %reduce-scatter.23.cloned.1.call-done = f32[729,432]{0,1:T(8,128)} async-done(((f32[729,1728]{0,1:T(8,128)}), f32[729,432]{0,1:T(8,128)}) %reduce-scatter.23.cloned.1.call-update) | async-done | bytes 1259728 | tf_op jit(solution)/shard_map/reduce_scatter | solution.py:51
  165.3 20.0 %all_gather.38 = bf16[729,576]{0,1:T(8,128)(2,1)S(1)} all-gather(bf16[729,144]{0,1:T(8,128)(2,1)S(1)} %bitcast.112), channel_id=1, replica_groups=mesh['dp'=4,'row'=4,'col'=2] {'row'}, dimensions={1}, use_global_device_ids=true | all-gather | bytes 1049760 | tf_op jit(solution)/shard_map/all_gather | solution.py:47
  192.3 3.3 copy.110
  198.0 5.8 fusion.81
  204.8 15.3 %psum.72 = f32[729]{0:T(1024)S(1)} all-reduce(f32[729]{0:T(1024)S(1)} %fusion.62), channel_id=1, replica_groups=mesh['dp'=4,'row'=4,'col'=2] {'row','col'}, use_global_device_ids=true, to_apply=%region_9.10 | all-reduce | flops 729 | bytes 5832 | tf_op jit(solution)/shard_map/psum | solution.py:61
  221.2 13.6 %psum.73 = f32[729]{0:T(1024)S(1)} all-reduce(f32[729]{0:T(1024)S(1)} %multiply_reduce_fusion.2), channel_id=1, replica_groups=mesh['dp'=4,'row'=4,'col'=2] {'row','col'}, use_global_device_ids=true, to_apply=%region_11.12 | all-reduce | flops 729 | bytes 5832 | tf_op jit(solution)/shard_map/psum | solution.py:63
  238.9 4.7 fusion.80
  243.6 225.3 %fusion.63 = (f32[729,544]{0,1:T(8,128)S(1)}, f32[729,544]{0,1:T(8,128)}) fusion(f32[729,2152]{0,1:T(8,128)} %fusion.80, f32[729,2152]{0,1:T(8,128)} %fusion.81), kind=kCustom, calls=%all-reduce-scatter.2 | all-reduce-scatter fusion | flops 3172609 | bytes 15723584
  479.0 7.2 concatenate.1
  486.2 6.0 concatenate
  492.2 5.4 convert_reduce_fusion
  498.0 64.7 %all-gather.16.cloned.1.call-done = bf16[4,538,729]{2,1,0:T(8,128)(2,1)} async-done(((bf16[1,538,729]{2,1,0:T(8,128)(2,1)}), bf16[4,538,729]{2,1,0:T(8,128)(2,1)}) %all-gather.16.cloned.1.call-update) | async-done | bytes 3137632 | tf_op jit(solution)/shard_map/all_gather | solution.py:47
  562.7 5.2 reshape.110
  568.0 3.9 convolution_convert_fusion.5
  572.0 6.6 reduce-scatter.29.cloned.1.call-done
  580.4 17.3 %all-reduce.10 = (f32[729]{0:T(1024)S(1)}, f32[729]{0:T(1024)S(1)}) all-reduce(f32[729]{0:T(1024)S(1)} %get-tuple-element.88, f32[729]{0:T(1024)S(1)} %get-tuple-element.92), channel_id=1, replica_groups=mesh['dp'=4,'row'=4,'col'=2] {'row','col'}, use_global_device_ids=true, to_apply=%region_19.20 | all-reduce | flops 1458 | bytes 11664 | tf_op jit(solution)/shard_map/psum | solution.py:71
  604.5 36.0 %reduce-scatter.31.cloned.1.call-done = f32[729,144]{0,1:T(8,128)} async-done(((f32[729,576]{0,1:T(8,128)}), f32[729,144]{0,1:T(8,128)}) %reduce-scatter.31.cloned.1.call-update) | async-done | bytes 419920 | tf_op jit(solution)/shard_map/reduce_scatter | solution.py:51
  641.6 3.6 multiply_reduce_fusion
  654.8 4.3 convolution_convert_fusion.1
  663.0 44.7 %all-gather.14.cloned.1.call-done = bf16[4,538,729]{2,1,0:T(8,128)(2,1)} async-done(((bf16[1,538,729]{2,1,0:T(8,128)(2,1)}), bf16[4,538,729]{2,1,0:T(8,128)(2,1)}) %all-gather.14.cloned.1.call-update) | async-done | bytes 3137632 | tf_op jit(solution)/shard_map/all_gather | solution.py:47
  707.8 5.3 reshape.108
  713.1 4.4 convolution_convert_fusion
  721.2 42.2 %all-gather.12.cloned.1.call-done = bf16[729,1728]{0,1:T(8,128)(2,1)} async-done(((bf16[729,432]{0,1:T(8,128)(2,1)}), bf16[729,1728]{0,1:T(8,128)(2,1)}) %all-gather.12.cloned.1.call-update) | async-done | bytes 2519440 | tf_op jit(solution)/shard_map/all_gather | solution.py:47
  763.4 3.8 convolution_convert_fusion.3
  767.3 3.9 convolution_convert_fusion.6
  792.7 14.2 %all-reduce.9 = (f32[729]{0:T(1024)S(1)}, f32[729]{0:T(1024)S(1)}) all-reduce(f32[729]{0:T(1024)S(1)} %get-tuple-element.90, f32[729]{0:T(1024)S(1)} %get-tuple-element.91), channel_id=1, replica_groups=mesh['dp'=4,'row'=4,'col'=2] {'row','col'}, use_global_device_ids=true, to_apply=%region_26.27 | all-reduce | flops 1458 | bytes 11664 | tf_op jit(solution)/shard_map/psum | solution.py:71
  810.1 39.0 %all-reduce.8 = (f32[2,1152]{1,0:T(2,128)S(1)}, f32[11216]{0:T(1024)S(1)}) all-reduce(f32[2,1152]{1,0:T(2,128)S(1)} %dynamic_update_slice.33, f32[11216]{0:T(1024)S(1)} %dynamic_update_slice.40), channel_id=1, replica_groups=mesh['dp'=4,'row'=4,'col'=2] {'dp','row','col'}, use_global_device_ids=true, to_apply=%region_33.34 | all-reduce | flops 13520 | bytes 108160 | tf_op jit(solution)/shard_map/psum | solution.py:275
  (283 shorter events, 101.7 us)
Async XLA Ops:
  8.0 151.8 %reduce-scatter.23.cloned.1.call-start = ((), (), s32[]{:S(2)}) async-start(), calls=%async_computation.10 | async-start | bytes 6635520 | tf_op jit(solution)/shard_map/reduce_scatter | solution.py:51
  44.1 159.7 %copy-start.40 = (f32[144]{0:T(256)}, f32[144]{0:T(256)S(1)}, u32[]{:S(2)}) copy-start(f32[144]{0:T(256)S(1)} %get-tuple-element.135) | copy-start | bytes 1732
  67.6 122.2 %all-gather.8.cloned.1.call-start = ((), (), s32[]{:S(2)}) async-start(), calls=%async_computation.12 | async-start | bytes 1566720 | tf_op jit(solution)/shard_map/all_gather | solution.py:190
  69.4 122.8 %all-gather.10.cloned.1.call-start = ((), (), s32[]{:S(2)}) async-start(), calls=%async_computation.13 | async-start | bytes 1566720 | tf_op jit(solution)/shard_map/all_gather | solution.py:191
  70.3 133.5 %reduce-scatter.25.cloned.1.call-start = ((), (), s32[]{:S(2)}) async-start(), calls=%async_computation.11 | async-start | bytes 663552 | tf_op jit(solution)/shard_map/reduce_scatter | solution.py:55
  82.5 102.8 %copy-start.20 = (bf16[576,288]{0,1:T(8,128)(2,1)}, bf16[576,288]{0,1:T(8,128)(2,1)S(1)}, u32[]{:S(2)}) copy-start(bf16[576,288]{0,1:T(8,128)(2,1)S(1)} %reshape.104) | copy-start | bytes 995332
  186.6 376.0 %all-gather.16.cloned.1.call-start = ((), (), s32[]{:S(2)}) async-start(), calls=%async_computation.20 | async-start | bytes 4177920 | tf_op jit(solution)/shard_map/all_gather | solution.py:47
  192.2 45.9 %copy-start.3 = (bf16[288,2152]{1,0:T(8,128)(2,1)}, bf16[288,2152]{1,0:T(8,128)(2,1)S(1)}, u32[]{:S(2)}) copy-start(bf16[288,2152]{1,0:T(8,128)(2,1)S(1)} %reshape.105) | copy-start | bytes 3718660
  470.5 8.5 collective-permute-start.1
  473.0 13.2 %collective-permute-start = (f32[729,18]{0,1:T(8,128)}, f32[729,18]{0,1:T(8,128)}, u32[]{:S(2)}, u32[]{:S(2)}) collective-permute-start(f32[729,18]{0,1:T(8,128)} %slice.42), channel_id=1, source_target_pairs={{0,2},{2,4},{4,6},{1,3},{3,5},{5,7},{8,10},{10,12},{12,14},{9,11},... | collective-permute-start | bytes 157472
  497.6 70.4 %copy-start.4 = (bf16[288,2152]{1,0:T(8,128)(2,1)S(1)}, bf16[288,2152]{1,0:T(8,128)(2,1)}, u32[]{:S(2)}) copy-start(bf16[288,2152]{1,0:T(8,128)(2,1)} %copy-done.3) | copy-start | bytes 3718660
  497.6 81.0 %reduce-scatter.29.cloned.1.call-start = ((), (), s32[]{:S(2)}) async-start(), calls=%async_computation.15 | async-start | bytes 663552 | tf_op jit(solution)/shard_map/reduce_scatter | solution.py:55
  571.9 68.6 %reduce-scatter.31.cloned.1.call-start = ((), (), s32[]{:S(2)}) async-start(), calls=%async_computation.16 | async-start | bytes 2211840 | tf_op jit(solution)/shard_map/reduce_scatter | solution.py:51
  603.8 37.8 %copy-start.6 = (bf16[729,432]{0,1:T(8,128)(2,1)S(1)}, bf16[729,432]{0,1:T(8,128)(2,1)}, u32[]{:S(2)}) copy-start(bf16[729,432]{0,1:T(8,128)(2,1)} %copy-done.5) | copy-start | bytes 1889572
  603.8 104.0 %all-gather.14.cloned.1.call-start = ((), (), s32[]{:S(2)}) async-start(), calls=%async_computation.19 | async-start | bytes 4177920 | tf_op jit(solution)/shard_map/all_gather | solution.py:47
  604.4 159.1 %all-gather.12.cloned.1.call-start = ((), (), s32[]{:S(2)}) async-start(), calls=%async_computation.17 | async-start | bytes 3317760 | tf_op jit(solution)/shard_map/all_gather | solution.py:47
  650.2 121.1 %reduce-scatter.37.cloned.1.call-start = ((), (), s32[]{:S(2)}) async-start(), calls=%async_computation.22 | async-start | bytes 460800
  654.7 120.6 %reduce-scatter.39.cloned.1.call-start = ((), (), s32[]{:S(2)}) async-start(), calls=%async_computation.23 | async-start | bytes 1566720
  662.8 50.3 %copy-start.17 = (bf16[729,288]{0,1:T(8,128)(2,1)S(1)}, bf16[729,288]{0,1:T(8,128)(2,1)}, u32[]{:S(2)}) copy-start(bf16[729,288]{0,1:T(8,128)(2,1)} %all_gather.44) | copy-start | bytes 1259716
  662.8 118.4 %reduce-scatter.41.cloned.1.call-start = ((), (), s32[]{:S(2)}) async-start(), calls=%async_computation.24 | async-start | bytes 1566720
  721.2 68.8 %reduce-scatter.33.cloned.1.call-start = ((), (), s32[]{:S(2)}) async-start(), calls=%async_computation.18 | async-start | bytes 663552 | tf_op jit(solution)/shard_map/reduce_scatter | solution.py:55
  767.2 39.8 %reduce-scatter.27.cloned.1.call-start = ((), (), s32[]{:S(2)}) async-start(), calls=%async_computation.14 | async-start | bytes 663552 | tf_op jit(solution)/shard_map/reduce_scatter | solution.py:55
  771.2 79.2 %reduce-scatter.35.cloned.1.call-start = ((), (), s32[]{:S(2)}) async-start(), calls=%async_computation.21 | async-start | bytes 1290240
  789.7 59.4 %copy-start.49 = (f32[2,1152]{1,0:T(2,128)S(1)}, f32[2,1152]{1,0:T(2,128)}, u32[]{:S(2)}) copy-start(f32[2,1152]{1,0:T(2,128)} %param.34) | copy-start | bytes 27652
  789.7 59.4 %copy-start.58 = (f32[2,1152]{1,0:T(2,128)S(1)}, f32[2,1152]{1,0:T(2,128)}, u32[]{:S(2)}) copy-start(f32[2,1152]{1,0:T(2,128)} %param.35) | copy-start | bytes 27652
  789.7 59.4 %copy-start.59 = (f32[2,1152]{1,0:T(2,128)S(1)}, f32[2,1152]{1,0:T(2,128)}, u32[]{:S(2)}) copy-start(f32[2,1152]{1,0:T(2,128)} %param.36) | copy-start | bytes 27652
  789.7 60.0 %copy-start.35 = (f32[11216]{0:T(1024)S(1)}, f32[11216]{0:T(1024)}, u32[]{:S(2)}) copy-start(f32[11216]{0:T(1024)} %param.37) | copy-start | bytes 134596
  789.7 60.0 %copy-start.43 = (f32[11216]{0:T(1024)S(1)}, f32[11216]{0:T(1024)}, u32[]{:S(2)}) copy-start(f32[11216]{0:T(1024)} %param.38) | copy-start | bytes 134596
  789.7 60.0 %copy-start.44 = (f32[11216]{0:T(1024)S(1)}, f32[11216]{0:T(1024)}, u32[]{:S(2)}) copy-start(f32[11216]{0:T(1024)} %param.39) | copy-start | bytes 134596
  789.7 60.7 %copy-start.12 = (f32[72,1,1728]{2,1,0:T(1,128)S(1)}, f32[72,1,1728]{2,1,0:T(1,128)}, u32[]{:S(2)}) copy-start(f32[72,1,1728]{2,1,0:T(1,128)} %param.22) | copy-start | bytes 1492996
  789.8 60.7 %copy-start.28 = (f32[72,1,1728]{2,1,0:T(1,128)S(1)}, f32[72,1,1728]{2,1,0:T(1,128)}, u32[]{:S(2)}) copy-start(f32[72,1,1728]{2,1,0:T(1,128)} %param.26) | copy-start | bytes 1492996
  789.8 60.7 %copy-start.29 = (f32[72,1,1728]{2,1,0:T(1,128)S(1)}, f32[72,1,1728]{2,1,0:T(1,128)}, u32[]{:S(2)}) copy-start(f32[72,1,1728]{2,1,0:T(1,128)} %param.30) | copy-start | bytes 1492996
  (54 other events, 531.6 us)
Sparse Core Ops, SparseCore 0:
  67.7 92.0 reduce-scatter.22
  186.8 7.4 reduce-scatter.24
  497.7 64.9 all-gather.15
  572.0 6.4 reduce-scatter.28
  603.9 36.5 reduce-scatter.30
  641.9 65.8 all-gather.13
  709.4 53.9 all-gather.11
Sparse Core Ops, SparseCore 1:
  70.5 25.4 all-gather.7
  98.3 28.1 all-gather.9
  654.8 23.0 reduce-scatter.36
  680.8 29.2 reduce-scatter.38
  721.2 27.7 reduce-scatter.40
  767.3 6.5 reduce-scatter.32
  776.6 8.9 reduce-scatter.26
  789.9 28.0 reduce-scatter.34
where the time goes:
time: 872 us; the launch traced here: 863 us
  blocking collectives  411 us (47%)
  waiting for transfers between devices  272 us (31%)
  local copies, waits for them, and re-layouts  76.1 us (9%)
  matrix products  49.2 us (6%)
  other arithmetic  31.5 us (4%)
  between operations  17.5 us (2%)
    unnamed x1, blocking collectives  225 us
    all_gather x3, waiting for transfers between devices, spread_out(): lax.all_gather(as_sent(operand), 'row', axis=1, tiled=True)  152 us
    reduce_scatter x2, waiting for transfers between devices, reduce_inner(): return lax.psum_scatter(term, 'row', scatter_dimension=1, tiled=True)  113 us
    unnamed x161, local copies, waits for them, and re-layouts  48.6 us
    dot_general x12, matrix products, contract(): lax.dot_general(left_side, right_side, (((left_dim,), (right_dim,)), ((),...  41.5 us
    psum x1, blocking collectives, shards(): lax.psum((gain_grad, bias_grad), ('dp', 'row', 'col'))  39 us
    psum x2, blocking collectives, norm_forward(): average = lax.psum(jnp.sum(operand, axis=1), ('row', 'col')) / D  33.4 us
    psum x2, blocking collectives, norm_backward(): lax.psum((jnp.sum(scaled, axis=1), jnp.sum(scaled * normed, axis=1)), ('r...  31.5 us
  transfers between devices with their start and end apart: 17, of which 6 were waited for; matrix products, arithmetic and copies ran while one was open for 12% of the time, Pallas kernels for 0%

commit v1 on v0

v1 whole, which is shorter than its diff:
```python
import jax
import jax.numpy as jnp
from jax import lax
from jax.sharding import PartitionSpec as P

D = 1152
FF = 4304
HEAD = 72
SEQ = 729
STEP = 10

NORM_EPS = 1e-06
ADAM_EPS = 1e-08
BETA_ONE = 0.9
BETA_TWO = 0.999
LOW = jnp.bfloat16


def dot(left, right, left_dim, right_dim, out=jnp.float32, precision=None):
    return lax.dot_general(
        left,
        right,
        (((left_dim,), (right_dim,)), ((), ())),
        precision=precision,
        preferred_element_type=out,
    )


def take(array, index, size):
    return lax.dynamic_slice_in_dim(array, index * size, size, axis=0)


def swap_cores(array):
    n_col = lax.axis_size("col")
    return lax.ppermute(array, "col", [(i, (i + 1) % n_col) for i in range(n_col)])


def gather_eight(block):
    rows = lax.all_gather(block, "row", axis=0, tiled=True)
    return lax.all_gather(rows, "col", axis=0, tiled=True)


def sum_over_rows(half):
    n_row = lax.axis_size("row")
    blocks = half.astype(LOW).reshape(n_row, half.shape[0] // n_row, half.shape[1])
    return jnp.sum(lax.all_to_all(blocks, "row", 0, 0).astype(jnp.float32), axis=0)


def reduce_eight(product):
    core = lax.axis_index("col")
    theirs = product(1 - core).astype(LOW)
    got = swap_cores(theirs)
    mine = product(core)
    return sum_over_rows(mine + got.astype(jnp.float32))


def exchange_rows(blocks):
    return lax.all_to_all(blocks, "row", 0, 0)


def all_sum(vector):
    for axis in ("col", "row", "dp"):
        size = lax.axis_size(axis)
        if size & (size - 1) or size > 4:
            vector = lax.psum(vector, axis)
            continue
        step = 1
        while step < size:
            vector = vector + lax.ppermute(vector, axis, [(i, i ^ step) for i in range(size)])
            step *= 2
    return vector


def attend_forward(queries, key_rows, values):
    scores = (
        jnp.einsum("hdq,hdk->hqk", queries, key_rows, preferred_element_type=jnp.float32)
        * HEAD ** (-0.5)
    )
    row_max = jnp.max(scores, axis=2, keepdims=True)
    exponent = jnp.exp(scores - row_max)
    row_total = jnp.sum(exponent, axis=2, keepdims=True)
    probs_low = (exponent / row_total).astype(LOW)
    attended = jnp.einsum("hqk,hdk->hdq", probs_low, values, preferred_element_type=jnp.float32)
    return attended.astype(LOW), row_max + jnp.log(row_total)


def attend_backward(queries, key_rows, values, log_total, attended_grad):
    scale = HEAD ** (-0.5)
    scores = (
        jnp.einsum("hdq,hdk->hqk", queries, key_rows, preferred_element_type=jnp.float32) * scale
    )
    probs = jnp.exp(scores - log_total)
    probs_low = probs.astype(LOW)
    value_grad = jnp.einsum(
        "hqk,hdq->hdk", probs_low, attended_grad, preferred_element_type=jnp.float32
    )
    probs_grad = jnp.einsum(
        "hdq,hdk->hqk", attended_grad, values, preferred_element_type=jnp.float32
    )
    inner = jnp.sum(probs * probs_grad, axis=2, keepdims=True)
    scores_grad = (probs * (probs_grad - inner)).astype(LOW)
    query_grad = (
        jnp.einsum("hqk,hdk->hdq", scores_grad, key_rows, preferred_element_type=jnp.float32)
        * scale
    )
    key_grad = (
        jnp.einsum("hqk,hdq->hdk", scores_grad, queries, preferred_element_type=jnp.float32) * scale
    )
    return jnp.stack([query_grad, key_grad, value_grad], axis=1).astype(LOW)


def adam_update(weights, moment_one, second, gradient, step_rate, weight_decay):
    moment_one = BETA_ONE * moment_one + (1.0 - BETA_ONE) * gradient
    second = BETA_TWO * second + (1.0 - BETA_TWO) * gradient * gradient
    direction = (
        moment_one / (1.0 - BETA_ONE**STEP) / (jnp.sqrt(second / (1.0 - BETA_TWO**STEP)) + ADAM_EPS)
    )
    return (weights - step_rate * (direction + weight_decay * weights), moment_one, second)


def shards(
    inputs,
    cotangent,
    qkv_master,
    out_master,
    up_master,
    down_master,
    qkv_first,
    out_first,
    up_first,
    down_first,
    qkv_second,
    out_second,
    up_second,
    down_second,
    norm_gains,
    gain_first,
    gain_second,
    biases,
    bias_first,
    bias_second,
):
    tokens, width = inputs.shape
    n_row = lax.axis_size("row")
    n_col = lax.axis_size("col")
    n_dp = lax.axis_size("dp")
    row = lax.axis_index("row")
    core = lax.axis_index("col")
    group = n_row * n_col
    heads = width // HEAD
    hidden_width = FF // group
    own = core * n_row + row
    chunk = -(-tokens // (group * 16)) * 16
    padded = chunk * group
    shard_rows = qkv_master.shape[0]

    place = lax.broadcasted_iota(jnp.int32, (D, D), 0)
    source = lax.broadcasted_iota(jnp.int32, (D, D), 1)
    feature = (
        ((place // width) % n_row) * n_col + place // (width * n_row)
    ) * width + place % width
    order = (source == (feature % n_dp) * (D // n_dp) + feature // n_dp).astype(LOW)

    def mixed(vector):
        return vector.reshape(n_row, n_col, width).transpose(1, 0, 2).reshape(D)

    def plain(vector):
        return vector.reshape(n_col, n_row, width).transpose(1, 0, 2).reshape(D)

    def to_owner(rows, parts):
        return rows.reshape(shard_rows, parts, -1).transpose(1, 0, 2)

    def gathered(blocks):
        flat = blocks.reshape(n_row * shard_rows, blocks.shape[2])
        return dot(order, lax.all_gather(flat, "dp", axis=0, tiled=True), 1, 0, LOW)

    def scattered(gradient):
        n = gradient.shape[1]
        rows = dot(order, gradient.astype(LOW), 0, 0, LOW)
        summed = lax.psum_scatter(rows, "dp", scatter_dimension=0, tiled=True)
        blocks = exchange_rows(summed.reshape(n_row, shard_rows, n))
        return blocks.astype(jnp.float32)

    def widened(blocks):
        return blocks.transpose(1, 0, 2).reshape(shard_rows, -1)

    x_all = gather_eight(inputs.T)
    w_qkv = gathered(exchange_rows(to_owner(qkv_master[:, 0].astype(LOW), n_row)))
    rest = jnp.concatenate(
        [
            to_owner(out_master[:, :, 0].T.astype(LOW), n_row),
            to_owner(up_master[:, 0].astype(LOW), n_row),
            to_owner(down_master[:, :, 0].T.astype(LOW), n_row),
        ],
        axis=2,
    )
    w_rest = gathered(exchange_rows(rest))
    w_out = w_rest[:, :width]
    w_up = w_rest[:, width : width + hidden_width]
    w_down = w_rest[:, width + hidden_width :]
    cot_all = gather_eight(cotangent.T)

    gain_one = mixed(norm_gains[0])
    gain_two = mixed(norm_gains[1])
    shift_one = mixed(biases[:D])
    shift_two = mixed(biases[D : 2 * D])
    query_bias = lax.dynamic_slice_in_dim(biases, 2 * D + own * width, width).reshape(heads, HEAD)
    value_bias = lax.dynamic_slice_in_dim(biases, 3 * D + own * width, width).reshape(heads, HEAD)
    out_bias = mixed(biases[4 * D : 5 * D])
    feature_start = (row * n_col + core) * width
    down_bias = lax.dynamic_slice_in_dim(biases, 5 * D + feature_start, width)
    up_bias = lax.dynamic_slice_in_dim(biases, 6 * D + own * hidden_width, hidden_width)
    qkv_bias = jnp.stack([query_bias, jnp.zeros_like(query_bias), value_bias], axis=1).reshape(
        3 * width, 1
    )

    x_full = x_all.astype(jnp.float32)
    center = x_full - jnp.sum(x_full, axis=0, keepdims=True) / D
    inverse_one = lax.rsqrt(jnp.sum(center * center, axis=0, keepdims=True) / D + NORM_EPS)
    za = (center * inverse_one * gain_one[:, None] + shift_one[:, None]).astype(LOW)

    qkv = (dot(w_qkv, za, 0, 0) + qkv_bias).astype(LOW).reshape(heads, 3, HEAD, tokens)
    queries, key_rows, values = qkv[:, 0], qkv[:, 1], qkv[:, 2]
    attended, log_total = attend_forward(queries, key_rows, values)
    attended = jnp.pad(attended.reshape(width, tokens), ((0, 0), (0, padded - tokens)))

    half = padded // n_col
    branch = reduce_eight(
        lambda c: dot(lax.dynamic_slice_in_dim(attended, c * half, half, axis=1), w_out, 0, 1)
    )
    token_start = own * chunk
    mine = (
        lax.broadcasted_iota(jnp.int32, (chunk, tokens), 1)
        == lax.broadcasted_iota(jnp.int32, (chunk, tokens), 0) + token_start
    ).astype(LOW)
    middle = dot(mine, x_all, 1, 1) + branch + out_bias[None, :]
    center = middle - jnp.sum(middle, axis=1, keepdims=True) / D
    inverse_two = lax.rsqrt(jnp.sum(center * center, axis=1, keepdims=True) / D + NORM_EPS)
    normed_two = center * inverse_two
    zb = gather_eight((normed_two * gain_two + shift_two).astype(LOW))

    hidden = dot(zb, w_up, 1, 0) + up_bias
    active_grad = dot(
        jnp.pad(cot_all, ((0, 0), (0, padded - tokens))), w_down, 0, 0
    )
    active, gelu_pullback = jax.vjp(lambda v: jax.nn.gelu(v, approximate=True), hidden)
    active = active.astype(LOW)
    hidden_grad = gelu_pullback(active_grad)[0].astype(LOW)

    two_grad = reduce_eight(lambda c: dot(take(hidden_grad, c, half), w_up, 1, 1))
    cot_mine = dot(mine, cot_all, 1, 1)
    scaled = two_grad * gain_two
    first_sum = jnp.sum(scaled, axis=1, keepdims=True) / D
    second_sum = jnp.sum(scaled * normed_two, axis=1, keepdims=True) / D
    middle_grad = cot_mine + inverse_two * (scaled - first_sum - normed_two * second_sum)
    branch_all = gather_eight(middle_grad.astype(LOW))
    gain_two_grad = jnp.sum(two_grad * normed_two, axis=0)
    shift_two_grad = jnp.sum(two_grad, axis=0)
    out_bias_grad = jnp.sum(middle_grad.astype(LOW), axis=0, dtype=jnp.float32)
    down_bias_grad = jnp.sum(cot_mine, axis=0)
    up_bias_grad = jnp.sum(hidden_grad, axis=0, dtype=jnp.float32)

    attended_grad = dot(w_out, branch_all, 0, 1, LOW)[:, :tokens].reshape(heads, HEAD, tokens)
    qkv_grad = attend_backward(queries, key_rows, values, log_total, attended_grad)
    bias_sums = jnp.sum(qkv_grad, axis=3, dtype=jnp.float32)
    qkv_grad = qkv_grad.reshape(3 * width, tokens)
    qkv_blocks = scattered(dot(za, qkv_grad, 1, 1, LOW))

    one_part = dot(w_qkv, qkv_grad, 1, 0)
    normed_one = (x_full - jnp.sum(x_full, axis=0, keepdims=True) / D) * inverse_one
    gain_one_grad = jnp.sum(one_part * normed_one, axis=1)
    shift_one_grad = jnp.sum(one_part, axis=1)
    scaled_part = one_part * gain_one[:, None]
    sums = jnp.stack(
        [jnp.sum(scaled_part, axis=0), jnp.sum(scaled_part * normed_one, axis=0)], axis=0
    )
    sums = jnp.pad(sums, ((0, 14), (0, 0)))
    one_rows = one_part.reshape(n_col, n_row, width, tokens)
    one_rows = jnp.concatenate(
        [one_rows, jnp.broadcast_to(sums, (n_col, n_row, 16, tokens))], axis=2
    ).astype(LOW).reshape(n_col, n_row * (width + 16), tokens)
    one_grad = reduce_eight(
        lambda c: lax.dynamic_index_in_dim(one_rows, c, 0, keepdims=False).astype(jnp.float32)
    )
    own_gain = lax.dynamic_slice_in_dim(norm_gains[0], feature_start, width)[:, None]
    own_input = inputs.T.astype(jnp.float32)
    own_normed = (own_input - jnp.sum(x_full, axis=0, keepdims=True) / D) * inverse_one
    own_middle = lax.dynamic_slice_in_dim(branch_all, own * width, width, axis=1)[:tokens].T
    input_grad = own_middle.astype(jnp.float32) + inverse_one * (
        one_grad[:width] * own_gain
        - one_grad[width : width + 1] / D
        - own_normed * (one_grad[width + 1 : width + 2] / D)
    )
    input_grad = input_grad.astype(LOW).T

    down_half = lambda c: dot(take(w_down, c, D // n_col), active, 1, 1)[:, :tokens] + dot(
        lax.dynamic_slice_in_dim(middle, c * (D // n_col), D // n_col, axis=1),
        mine.astype(jnp.float32),
        0,
        0,
        precision=lax.Precision.HIGHEST,
    )
    result = (reduce_eight(down_half) + down_bias[:, None]).astype(LOW).T

    down_blocks = scattered(dot(jnp.pad(cot_all, ((0, 0), (0, padded - tokens))), active, 1, 0, LOW))
    up_blocks = scattered(dot(zb, hidden_grad, 0, 0, LOW))
    out_blocks = scattered(dot(branch_all, attended, 0, 1, LOW))

    gain_grad = jnp.stack([plain(gain_one_grad), plain(gain_two_grad)])
    zeros = jnp.zeros(biases.shape, jnp.float32)
    bias_grad = jnp.concatenate(
        [
            plain(shift_one_grad),
            plain(shift_two_grad),
            jnp.zeros((2 * D,), jnp.float32),
            plain(out_bias_grad),
            plain(down_bias_grad),
            jnp.zeros((FF,), jnp.float32),
        ]
    )
    bias_grad = lax.dynamic_update_slice_in_dim(
        bias_grad, bias_sums[:, 0].reshape(width), 2 * D + own * width, 0
    )
    bias_grad = lax.dynamic_update_slice_in_dim(
        bias_grad, bias_sums[:, 2].reshape(width), 3 * D + own * width, 0
    )
    bias_grad = lax.dynamic_update_slice_in_dim(
        bias_grad, up_bias_grad, 6 * D + own * hidden_width, 0
    )
    total = all_sum(jnp.concatenate([gain_grad.reshape(-1), bias_grad]))
    gain_total = total[: 2 * D].reshape(2, D)
    bias_total = total[2 * D :]

    q_new = adam_update(
        qkv_master, qkv_first, qkv_second, widened(qkv_blocks)[:, None], 0.03, 0.1
    )
    o_new = adam_update(
        out_master, out_first, out_second, widened(out_blocks).T[:, :, None], 0.12, 0.1
    )
    u_new = adam_update(up_master, up_first, up_second, widened(up_blocks)[:, None], 0.03, 0.1)
    d_new = adam_update(
        down_master, down_first, down_second, widened(down_blocks).T[:, :, None], 0.02, 0.1
    )
    g_new = adam_update(norm_gains, gain_first, gain_second, gain_total, 0.5, 0.0)
    b_new = adam_update(biases, bias_first, bias_second, bias_total, 0.5, 0.0)
    return (result, input_grad, *q_new, *o_new, *u_new, *d_new, *g_new, *b_new)


def solution(mesh):
    token_spec = P("dp", ("row", "col"))
    wide = P("row", "dp", "col")
    tall = P("col", "row", "dp")
    return jax.shard_map(
        shards,
        mesh=mesh,
        in_specs=(token_spec,) * 2 + (wide, tall, wide, tall) * 3 + (P(),) * 6,
        out_specs=(token_spec,) * 2
        + (wide,) * 3
        + (tall,) * 3
        + (wide,) * 3
        + (tall,) * 3
        + (P(),) * 6,
        check_vma=False,
    )
```

time: 872 us -> 460 us (0.53)
  blocking collectives: 411 us -> 101 us
  waiting for transfers between devices: 272 us -> 127 us
  local copies, waits for them, and re-layouts: 76.1 us -> 31.9 us
  starting transfers between devices: 5.83 us -> 48.6 us
  matrix products: 49.2 us -> 91.3 us
    unnamed x1 -> x0, blocking collectives: 225 us -> none
    psum x7 -> x0, blocking collectives: 131 us -> none  [the longest x1 39 us: shards(): lax.psum((gain_grad, bias_grad), ('dp', 'row', 'col'))]
    all_gather x5, waiting for transfers between devices: 152 us -> 28.6 us  [the longest x1 28.6 us: gathered(): return dot(order, lax.all_gather(flat, 'dp', axis=0, tiled=True), 1, 0, LOW)]
    reduce_scatter x6 -> x3, waiting for transfers between devices: 120 us -> 10.8 us  [scattered(): summed = lax.psum_scatter(rows, 'dp', scatter_dimension=0, tiled=True)]
    all_to_all x0 -> x10, waiting for transfers between devices: none -> 62.9 us  [the longest x4 53.2 us: sum_over_rows(): lax.all_to_all(blocks, 'row', 0, 0).astype(jnp.float32)]
    all_gather x7 -> x5, blocking collectives: 54.4 us -> 101 us  [the longest x4 86.1 us: gather_eight(): rows = lax.all_gather(block, 'row', axis=0, tiled=True)]
    unnamed x161 -> x118, local copies, waits for them, and re-layouts: 48.6 us -> 6.22 us
    all_to_all x0 -> x10, starting transfers between devices: none -> 41.6 us  [the longest x6 25.6 us: exchange_rows(): return lax.all_to_all(blocks, 'row', 0, 0)]
  transfers between devices with their start and end apart: 17 -> 28, of which waited for: 6 -> 13; matrix products, arithmetic and copies ran while one was open for 12% -> 26% of each run, Pallas kernels for 0% -> 0%
where the time goes in v1:
time: 460 us; the launch traced here: 454 us
  waiting for transfers between devices  127 us (28%)
  blocking collectives  101 us (22%)
  matrix products  91.3 us (20%)
  starting transfers between devices  48.6 us (11%)
  other arithmetic  39.1 us (8%)
  local copies, waits for them, and re-layouts  31.9 us (7%)
  between operations  15.6 us (3%)
    all_gather x4, blocking collectives, gather_eight(): rows = lax.all_gather(block, 'row', axis=0, tiled=True)  86.1 us
    dot_general x17, matrix products, dot(): lax.dot_general(left, right, (((left_dim,), (right_dim,)), ((), ())), pre...  55.9 us
    all_to_all x4, waiting for transfers between devices, sum_over_rows(): lax.all_to_all(blocks, 'row', 0, 0).astype(jnp.float32)  53.2 us
    all_gather x1, waiting for transfers between devices, gathered(): return dot(order, lax.all_gather(flat, 'dp', axis=0, tiled=True), 1, 0, LOW)  28.6 us
    all_to_all x6, starting transfers between devices, exchange_rows(): return lax.all_to_all(blocks, 'row', 0, 0)  25.6 us
    unnamed x4, matrix products  25.4 us
    sub x6, other arithmetic, adam_update(): weights - step_rate * (direction + weight_decay * weights)  20.9 us
    unnamed x10, waiting for transfers between devices  19.5 us
  transfers between devices with their start and end apart: 28, of which 13 were waited for; matrix products, arithmetic and copies ran while one was open for 26% of the time, Pallas kernels for 0%

profile of v1, /device:TPU:0, one launch (start us, length us, event | category | flops | bytes accessed | tf_op | source)
XLA Modules:
  0.0 453.7 jit_solution(4418573903416292714)
XLA Ops:
  10.9 6.3 %all-to-all-start.1 = ((bf16[4,72,432]{2,1,0:T(8,128)(2,1)}), bf16[4,72,432]{2,1,0:T(8,128)(2,1)S(1)}, u32[]{:S(2)}, u32[]{:S(2)}) async-start(bf16[4,72,432]{2,1,0:T(8,128)(2,1)} %copy.124), calls=%async_computation.1 | async-start | bytes 589824 | tf_op jit(solution)/shard_map/all_to_all | solution.py:58
  17.3 24.8 %all_gather.31 = bf16[576,729]{1,0:T(8,128)(2,1)} all-gather(bf16[144,729]{1,0:T(8,128)(2,1)} %bitcast.169), channel_id=1, replica_groups=mesh['dp'=4,'row'=4,'col'=2] {'row'}, dimensions={0}, use_global_device_ids=true | all-gather | bytes 1049760 | tf_op jit(solution)/shard_map/all_gather | solution.py:39
  48.3 3.7 all-to-all-start
  53.2 14.6 %all_gather.33 = bf16[1152,432]{1,0:T(8,128)(2,1)S(1)} all-gather(bf16[288,432]{1,0:T(8,128)(2,1)S(1)} %bitcast.161), channel_id=1, replica_groups=mesh['dp'=4,'row'=4,'col'=2] {'dp'}, dimensions={0}, use_global_device_ids=true | all-gather | bytes 1244160 | tf_op jit(solution)/shard_map/all_gather | solution.py:175
  68.6 4.6 %fusion.150 = bf16[1152,432]{0,1:T(8,128)(2,1)S(1)} fusion(bf16[1152,432]{1,0:T(8,128)(2,1)S(1)} %all_gather.33, s32[1152]{0:T(1024)S(1)} %get-tuple-element.160, s32[1152]{0:T(1024)S(1)} %get-tuple-element.161, s32[1152]{0:T(1024)S(1)} %get-tuple-element.158, s32[1152]{0:T(1024)S(1)} %get-tuple-element.164, s32[1152]{0:T(1024)S(1)} %get-tuple-element.159, ...), kind=kOutput, calls=%fused_computation.247 | convolution fusion | flops 1199702016 | bytes 2021760 | tf_op jit(solution)/shard_map/dot_general | solution.py:20
  83.1 28.6 %all-gather.6.cloned.1.call-done = bf16[1152,1220]{1,0:T(8,128)(2,1)} async-done(((bf16[288,1220]{1,0:T(8,128)(2,1)}), bf16[1152,1220]{1,0:T(8,128)(2,1)}) %all-gather.6.cloned.1.call-update) | async-done | bytes 2810896 | tf_op jit(solution)/shard_map/all_gather | solution.py:175
  111.6 9.9 %fusion.152 = bf16[1152,1220]{0,1:T(8,128)(2,1)S(1)} fusion(bf16[1152,1220]{1,0:T(8,128)(2,1)} %all-gather.6.cloned.1.call-done, s32[1152]{0:T(1024)S(1)} %get-tuple-element.160, s32[1152]{0:T(1024)S(1)} %get-tuple-element.161, s32[1152]{0:T(1024)S(1)} %get-tuple-element.158, s32[1152]{0:T(1024)S(1)} %get-tuple-element.164, ...), kind=kOutput, calls=%fused_computation.248 | convolution fusion | flops 3291217920 | bytes 5652864 | tf_op jit(solution)/shard_map/dot_general | solution.py:20
  129.5 4.6 %all-to-all-start.2 = ((bf16[4,96,1152]{2,1,0:T(8,128)(2,1)}), bf16[4,96,1152]{2,1,0:T(8,128)(2,1)S(1)}, u32[]{:S(2)}, u32[]{:S(2)}) async-start(bf16[4,96,1152]{2,1,0:T(8,128)(2,1)} %bitcast.17), calls=%async_computation.2 | async-start | bytes 1769472 | tf_op jit(solution)/shard_map/all_to_all | solution.py:46
  134.7 21.9 %all-to-all-done.2 = bf16[4,96,1152]{2,1,0:T(8,128)(2,1)S(1)} async-done(((bf16[4,96,1152]{2,1,0:T(8,128)(2,1)}), bf16[4,96,1152]{2,1,0:T(8,128)(2,1)S(1)}, u32[]{:S(2)}, u32[]{:S(2)}) %all-to-all-start.2) | async-done | bytes 884768 | tf_op jit(solution)/shard_map/all_to_all | solution.py:46
  159.4 19.4 %all_gather.34 = bf16[384,1152]{1,0:T(8,128)(2,1)} all-gather(bf16[96,1152]{1,0:T(8,128)(2,1)S(1)} %add_convert_fusion.6), channel_id=1, replica_groups=mesh['dp'=4,'row'=4,'col'=2] {'row'}, dimensions={0}, use_global_device_ids=true | all-gather | bytes 1105920 | tf_op jit(solution)/shard_map/all_gather | solution.py:39
  178.9 19.1 %all_gather.36 = bf16[576,729]{1,0:T(8,128)(2,1)} all-gather(bf16[144,729]{1,0:T(8,128)(2,1)S(1)} %bitcast.177), channel_id=1, replica_groups=mesh['dp'=4,'row'=4,'col'=2] {'row'}, dimensions={0}, use_global_device_ids=true | all-gather | bytes 1049760 | tf_op jit(solution)/shard_map/all_gather | solution.py:39
  204.3 5.0 %multiply_convert_fusion.1 = (bf16[768,538]{0,1:T(8,128)(2,1)S(1)}, f32[768,538]{0,1:T(8,128)}) fusion(f32[538]{0:T(1024)S(1)} %dynamic_slice.54, bf16[768,1152]{1,0:T(8,128)(2,1)} %all-gather.10.cloned.1.call-done, bf16[1152,1220]{0,1:T(8,128)(2,1)} %copy-done.13), kind=kOutput, calls=%fused_computation.85 | convolution fusion | flops 956107776 | bytes 5504104 | tf_op jit(solution)/shard_map/dot_general | solution.py:20
  211.4 5.3 %convert_reduce_fusion.6 = (f32[538]{0:T(1024)}, bf16[768,538]{0,1:T(8,128)(2,1)S(1)}) fusion(f32[768,538]{0,1:T(8,128)} %get-tuple-element.154, f32[538]{0:T(1024)S(1)} %dynamic_slice.54, bf16[1152,1220]{0,1:T(8,128)(2,1)} %copy-done.13, bf16[1152,729]{1,0:T(8,128)(2,1)} %all-gather.12.cloned.1.call-done), kind=kOutput, calls=%fused_computation.84 | convolution fusion | flops 961478656 | bytes 5524688 | tf_op jit(solution)/shard_map/dot_general | solution.py:20
  224.0 3.6 all-to-all-start.3
  227.9 6.9 %fusion.32 = bf16[1152,538]{1,0:T(8,128)(2,1)} fusion(bf16[768,538]{0,1:T(8,128)(2,1)} %copy-done.17, bf16[1152,729]{1,0:T(8,128)(2,1)} %all-gather.12.cloned.1.call-done, s32[1152]{0:T(1024)S(1)} %get-tuple-element.160, s32[1152]{0:T(1024)S(1)} %get-tuple-element.161, s32[1152]{0:T(1024)S(1)} %get-tuple-element.158, s32[1152]{0:T(1024)S(1)} %get-tuple-element.164, ...), kind=kOutput, calls=%fused_computation.49 | convolution fusion | flops 2434970880 | bytes 3776640
  238.4 11.8 %all-to-all-done.3 = bf16[4,144,729]{2,1,0:T(8,128)(2,1)S(1)} async-done(((bf16[4,144,729]{2,1,0:T(8,128)(2,1)}), bf16[4,144,729]{2,1,0:T(8,128)(2,1)S(1)}, u32[]{:S(2)}, u32[]{:S(2)}) %all-to-all-start.3) | async-done | bytes 839840 | tf_op jit(solution)/shard_map/all_to_all | solution.py:46
  250.2 4.2 all-to-all-start.4
  254.6 7.0 %fusion.29 = bf16[1152,538]{1,0:T(8,128)(2,1)} fusion(bf16[768,1152]{1,0:T(8,128)(2,1)} %all-gather.10.cloned.1.call-done, bf16[768,538]{0,1:T(8,128)(2,1)} %copy-done.49, s32[1152]{0:T(1024)S(1)} %get-tuple-element.160, s32[1152]{0:T(1024)S(1)} %get-tuple-element.161, s32[1152]{0:T(1024)S(1)} %get-tuple-element.158, s32[1152]{0:T(1024)S(1)} %get-tuple-element.164, ...), kind=kOutput, calls=%fused_computation.48 | convolution fusion | flops 2434970880 | bytes 3866496
  264.0 12.2 %all-to-all-done.4 = bf16[4,96,1152]{2,1,0:T(8,128)(2,1)} async-done(((bf16[4,96,1152]{2,1,0:T(8,128)(2,1)}), bf16[4,96,1152]{2,1,0:T(8,128)(2,1)}, u32[]{:S(2)}, u32[]{:S(2)}) %all-to-all-start.4) | async-done | bytes 884768 | tf_op jit(solution)/shard_map/all_to_all | solution.py:46
  284.6 22.8 %all_gather.38 = bf16[384,1152]{1,0:T(8,128)(2,1)} all-gather(bf16[96,1152]{1,0:T(8,128)(2,1)S(1)} %get-tuple-element.122), channel_id=1, replica_groups=mesh['dp'=4,'row'=4,'col'=2] {'row'}, dimensions={0}, use_global_device_ids=true | all-gather | bytes 1105920 | tf_op jit(solution)/shard_map/all_gather | solution.py:39
  307.5 4.0 all-to-all-start.8
  313.7 5.1 %multiply_subtract_fusion = (f32[2152,72,1]{0,2,1:T(1,128)}, f32[2152,72,1]{0,2,1:T(1,128)}, f32[2152,72,1]{0,2,1:T(1,128)}) fusion(f32[2152,72,1]{0,2,1:T(1,128)S(1)} %copy-done.4, f32[2152,72,1]{0,1,2:T(8,128)S(1)} %bitcast_add_fusion.1, f32[2152,72]{0,1:T(8,128)S(1)} %multiply_multiply_fusion.2, f32[2152,72,1]{0,2,1:T(1,128)S(1)} %copy-done.23), kind=kLoop, calls=%fused_computation.124 | loop fusion | flops 1549440 | bytes 4338432 | tf_op jit(solution)/shard_map/sub | solution.py:118
  321.2 6.5 %multiply_subtract_fusion.1 = (f32[72,1,2152]{2,1,0:T(1,128)}, f32[72,1,2152]{2,1,0:T(1,128)}, f32[72,1,2152]{2,1,0:T(1,128)}) fusion(f32[72,1,2152]{2,1,0:T(1,128)S(1)} %copy-done.6, f32[72,1,2152]{2,1,0:T(1,128)} %reshape.328, f32[72,1,2152]{2,1,0:T(1,128)} %param.28, f32[72,1,2152]{2,1,0:T(1,128)} %param.32), kind=kLoop, calls=%fused_computation.126 | loop fusion | flops 2324160 | bytes 4338432 | tf_op jit(solution)/shard_map/sub | solution.py:118
  358.0 5.6 %fusion.68 = bf16[1152,144]{1,0:T(8,128)(2,1)} fusion(bf16[768,1152]{1,0:T(8,128)(2,1)} %all-gather.14.cloned.1.call-done, bf16[144,729]{1,0:T(8,128)(2,1)S(1)} %bitcast.168, s32[1152]{0:T(1024)S(1)} %get-tuple-element.160, s32[1152]{0:T(1024)S(1)} %get-tuple-element.161, s32[1152]{0:T(1024)S(1)} %copy-done.33, s32[1152]{0:T(1024)S(1)} %copy-done.37, ...), kind=kOutput, calls=%fused_computation.100 | convolution fusion | flops 690094080 | bytes 2342304
  363.9 5.8 %fusion.35 = bf16[1152,432]{1,0:T(8,128)(2,1)} fusion(bf16[1152,729]{0,1:T(8,128)(2,1)} %copy-done.11, bf16[432,729]{1,0:T(8,128)(2,1)S(1)} %bitcast.171, s32[1152]{0:T(1024)S(1)} %get-tuple-element.160, s32[1152]{0:T(1024)S(1)} %get-tuple-element.161, s32[1152]{0:T(1024)S(1)} %copy-done.33, s32[1152]{0:T(1024)S(1)} %copy-done.37, s32[1152]{0:T(1024)S(1)} %copy-done.35, ...), kind=kOutput, calls=%fused_computation.51 | convolution fusion | flops 1927120896 | bytes 3335904
  369.9 19.3 %reduce-scatter.13.cloned.1.call-done = bf16[288,144]{1,0:T(8,128)(2,1)} async-done(((bf16[1152,144]{1,0:T(8,128)(2,1)}), bf16[288,144]{1,0:T(8,128)(2,1)}) %reduce-scatter.13.cloned.1.call-update) | async-done | bytes 82960
  390.9 4.6 %all-to-all-start.7 = ((bf16[4,72,144]{1,2,0:T(8,128)(2,1)}), bf16[4,72,144]{1,2,0:T(8,128)(2,1)S(1)}, u32[]{:S(2)}, u32[]{:S(2)}) async-start(bf16[4,72,144]{1,2,0:T(8,128)(2,1)} %copy.145), calls=%async_computation.8 | async-start | bytes 294912 | tf_op jit(solution)/shard_map/all_to_all | solution.py:58
  410.2 10.7 %reduce-scatter.7.cloned.1.call-done = bf16[288,432]{1,0:T(8,128)(2,1)} async-done(((bf16[1152,432]{1,0:T(8,128)(2,1)}), bf16[288,432]{1,0:T(8,128)(2,1)}) %reduce-scatter.7.cloned.1.call-update) | async-done | bytes 248848 | tf_op jit(solution)/shard_map/reduce_scatter | solution.py:180
  420.9 7.3 %all-to-all-done.5 = bf16[4,160,729]{2,1,0:T(8,128)(2,1)S(1)} async-done(((bf16[4,160,729]{2,1,0:T(8,128)(2,1)}), bf16[4,160,729]{2,1,0:T(8,128)(2,1)S(1)}, u32[]{:S(2)}, u32[]{:S(2)}) %all-to-all-start.5) | async-done | bytes 933152 | tf_op jit(solution)/shard_map/all_to_all | solution.py:46
  428.2 3.6 all-to-all-start.6
  434.9 6.0 %all-to-all-done.6 = bf16[4,72,432]{2,1,0:T(8,128)(2,1)S(1)} async-done(((bf16[4,72,432]{2,1,0:T(8,128)(2,1)}), bf16[4,72,432]{2,1,0:T(8,128)(2,1)S(1)}, u32[]{:S(2)}, u32[]{:S(2)}) %all-to-all-start.6) | async-done | bytes 248864 | tf_op jit(solution)/shard_map/all_to_all | solution.py:58
  442.3 4.6 %multiply_subtract_fusion.2 = (f32[72,1,1728]{2,1,0:T(1,128)}, f32[72,1,1728]{2,1,0:T(1,128)}, f32[72,1,1728]{2,1,0:T(1,128)}) fusion(f32[72,1,1728]{2,1,0:T(1,128)S(1)} %copy-done.7, f32[72,1,1728]{2,1,0:T(1,128)S(1)} %reshape.327, f32[72,1,1728]{2,1,0:T(1,128)S(1)} %copy-done.24, f32[72,1,1728]{2,1,0:T(1,128)S(1)} %copy-done.25), kind=kLoop, calls=%fused_computation.131 | loop fusion | flops 1866240 | bytes 3483648 | tf_op jit(solution)/shard_map/sub | solution.py:118
  (321 shorter events, 118.9 us)
Async XLA Ops:
  10.9 37.4 %all-to-all-start.1 = ((bf16[4,72,432]{2,1,0:T(8,128)(2,1)}), bf16[4,72,432]{2,1,0:T(8,128)(2,1)S(1)}, u32[]{:S(2)}, u32[]{:S(2)}) async-start(bf16[4,72,432]{2,1,0:T(8,128)(2,1)} %copy.124), calls=%async_computation.1 | async-start | bytes 589824 | tf_op jit(solution)/shard_map/all_to_all | solution.py:58
  17.3 56.0 %all-gather.8.cloned.1.call-start = ((), (), s32[]{:S(2)}) async-start(), calls=%async_computation.15 | async-start | bytes 2654208 | tf_op jit(solution)/shard_map/all_gather | solution.py:40
  48.3 19.4 %all-to-all-start = ((bf16[4,72,1220]{2,1,0:T(8,128)(2,1)}), bf16[4,72,1220]{2,1,0:T(8,128)(2,1)S(1)}, u32[]{:S(2)}, u32[]{:S(2)}) async-start(bf16[4,72,1220]{2,1,0:T(8,128)(2,1)} %copy.121), calls=%async_computation | async-start | bytes 1474560 | tf_op jit(solution)/shard_map/all_to_all | solution.py:58
  52.0 59.7 %all-gather.6.cloned.1.call-start = ((), (), s32[]{:S(2)}) async-start(), calls=%async_computation.14 | async-start | bytes 3686400 | tf_op jit(solution)/shard_map/all_gather | solution.py:175
  53.0 201.5 %copy-start.43 = (pred[1152]{0:T(1024)(128)(4,1)}, pred[1152]{0:T(1024)(128)(4,1)S(1)}, u32[]{:S(2)}) copy-start(pred[1152]{0:T(1024)(128)(4,1)S(1)} %fusion.123) | copy-start | bytes 3460
  53.1 201.5 %copy-start.45 = (pred[1152]{0:T(1024)(128)(4,1)}, pred[1152]{0:T(1024)(128)(4,1)S(1)}, u32[]{:S(2)}) copy-start(pred[1152]{0:T(1024)(128)(4,1)S(1)} %get-tuple-element.162) | copy-start | bytes 3460
  53.1 201.4 %copy-start.47 = (pred[1152]{0:T(1024)(128)(4,1)}, pred[1152]{0:T(1024)(128)(4,1)S(1)}, u32[]{:S(2)}) copy-start(pred[1152]{0:T(1024)(128)(4,1)S(1)} %get-tuple-element.163) | copy-start | bytes 3460
  53.1 201.4 %copy-start.32 = (s32[1152]{0:T(1024)}, s32[1152]{0:T(1024)S(1)}, u32[]{:S(2)}) copy-start(s32[1152]{0:T(1024)S(1)} %get-tuple-element.158) | copy-start | bytes 13828
  124.5 2.6 collective-permute-start
  129.5 27.1 %all-to-all-start.2 = ((bf16[4,96,1152]{2,1,0:T(8,128)(2,1)}), bf16[4,96,1152]{2,1,0:T(8,128)(2,1)S(1)}, u32[]{:S(2)}, u32[]{:S(2)}) async-start(bf16[4,96,1152]{2,1,0:T(8,128)(2,1)} %bitcast.17), calls=%async_computation.2 | async-start | bytes 1769472 | tf_op jit(solution)/shard_map/all_to_all | solution.py:46
  134.1 70.2 %all-gather.10.cloned.1.call-start = ((), (), s32[]{:S(2)}) async-start(), calls=%async_computation.16 | async-start | bytes 2654208 | tf_op jit(solution)/shard_map/all_gather | solution.py:40
  178.9 32.5 %all-gather.12.cloned.1.call-start = ((), (), s32[]{:S(2)}) async-start(), calls=%async_computation.17 | async-start | bytes 2654208 | tf_op jit(solution)/shard_map/all_gather | solution.py:40
  211.4 9.3 %collective-permute-start.1 = (bf16[576,729]{1,0:T(8,128)(2,1)}, bf16[576,729]{1,0:T(8,128)(2,1)}, u32[]{:S(2)}, u32[]{:S(2)}) collective-permute-start(bf16[576,729]{1,0:T(8,128)(2,1)} %add_convert_fusion.2), channel_id=1, source_target_pairs={{0,1},{1,0},{2,3},{3,2},{4,5},{5,4},{6,7},{7,6},{8,9},{9,8},{10,11... | collective-permute-start | bytes 2519432 | tf_op jit(solution)/shard_map/ppermute | solution.py:35
  220.2 14.7 %collective-permute-start.2 = (bf16[384,1152]{1,0:T(8,128)(2,1)}, bf16[384,1152]{1,0:T(8,128)(2,1)}, u32[]{:S(2)}, u32[]{:S(2)}) collective-permute-start(bf16[384,1152]{1,0:T(8,128)(2,1)} %convolution_convert_fusion.1), channel_id=1, source_target_pairs={{0,1},{1,0},{2,3},{3,2},{4,5},{5,4},{6,7},{7,6},{8,9},{9,8},{10,11... | collective-permute-start | bytes 2654216 | tf_op jit(solution)/shard_map/ppermute | solution.py:35
  224.0 26.1 %all-to-all-start.3 = ((bf16[4,144,729]{2,1,0:T(8,128)(2,1)}), bf16[4,144,729]{2,1,0:T(8,128)(2,1)S(1)}, u32[]{:S(2)}, u32[]{:S(2)}) async-start(bf16[4,144,729]{2,1,0:T(8,128)(2,1)} %bitcast.149), calls=%async_computation.3 | async-start | bytes 1769472 | tf_op jit(solution)/shard_map/all_to_all | solution.py:46
  227.7 50.4 %reduce-scatter.11.cloned.1.call-start = ((), (), s32[]{:S(2)}) async-start(), calls=%async_computation.21 | async-start | bytes 1843200 | tf_op jit(solution)/shard_map/reduce_scatter | solution.py:180
  250.2 26.1 %all-to-all-start.4 = ((bf16[4,96,1152]{2,1,0:T(8,128)(2,1)}), bf16[4,96,1152]{2,1,0:T(8,128)(2,1)}, u32[]{:S(2)}, u32[]{:S(2)}) async-start(bf16[4,96,1152]{2,1,0:T(8,128)(2,1)} %bitcast.165), calls=%async_computation.4 | async-start | bytes 1769472 | tf_op jit(solution)/shard_map/all_to_all | solution.py:46
  254.4 53.0 %reduce-scatter.9.cloned.1.call-start = ((), (), s32[]{:S(2)}) async-start(), calls=%async_computation.20 | async-start | bytes 1843200 | tf_op jit(solution)/shard_map/reduce_scatter | solution.py:180
  278.1 29.4 %all-to-all-start.9 = ((bf16[4,72,538]{2,1,0:T(8,128)(2,1)}), bf16[4,72,538]{2,1,0:T(8,128)(2,1)S(1)}, u32[]{:S(2)}, u32[]{:S(2)}) async-start(bf16[4,72,538]{2,1,0:T(8,128)(2,1)} %bitcast.173), calls=%async_computation.12 | async-start | bytes 737280 | tf_op jit(solution)/shard_map/all_to_all | solution.py:58
  281.5 46.2 %all-gather.14.cloned.1.call-start = ((), (), s32[]{:S(2)}) async-start(), calls=%async_computation.18 | async-start | bytes 2654208 | tf_op jit(solution)/shard_map/all_gather | solution.py:40
  307.5 11.6 %all-to-all-start.8 = ((bf16[4,72,538]{2,1,0:T(8,128)(2,1)}), bf16[4,72,538]{2,1,0:T(8,128)(2,1)S(1)}, u32[]{:S(2)}, u32[]{:S(2)}) async-start(bf16[4,72,538]{2,1,0:T(8,128)(2,1)} %bitcast.174), calls=%async_computation.10 | async-start | bytes 737280 | tf_op jit(solution)/shard_map/all_to_all | solution.py:58
  311.4 77.8 %reduce-scatter.13.cloned.1.call-start = ((), (), s32[]{:S(2)}) async-start(), calls=%async_computation.22 | async-start | bytes 737280
  344.1 2.4 collective-permute-start.4
  346.5 4.4 collective-permute-start.5
  350.9 5.6 %collective-permute-start.6 = (f32[13520]{0:T(1024)S(1)}, f32[13520]{0:T(1024)S(1)}, u32[]{:S(2)}, u32[]{:S(2)}) collective-permute-start(f32[13520]{0:T(1024)S(1)} %add.486), channel_id=1, source_target_pairs={{0,4},{2,6},{4,0},{6,2},{1,5},{3,7},{5,1},{7,3},{8,12},{10,14},{12... | collective-permute-start | bytes 162248 | tf_op jit(solution)/shard_map/ppermute | solution.py:69
  354.9 40.6 %collective-permute-start.3 = (bf16[640,729]{0,1:T(8,128)(2,1)}, bf16[640,729]{0,1:T(8,128)(2,1)}, u32[]{:S(2)}, u32[]{:S(2)}) collective-permute-start(bf16[640,729]{0,1:T(8,128)(2,1)} %bitcast.162), channel_id=1, source_target_pairs={{0,1},{1,0},{2,3},{3,2},{4,5},{5,4},{6,7},{7,6},{8,9},{9,8},{10,11... | collective-permute-start | bytes 2799368 | tf_op jit(solution)/shard_map/ppermute | solution.py:35
  356.5 7.2 %collective-permute-start.7 = (f32[13520]{0:T(1024)S(1)}, f32[13520]{0:T(1024)S(1)}, u32[]{:S(2)}, u32[]{:S(2)}) collective-permute-start(f32[13520]{0:T(1024)S(1)} %add.487), channel_id=1, source_target_pairs={{0,8},{8,0},{16,24},{24,16},{1,9},{9,1},{17,25},{25,17},{2,10},{10... | collective-permute-start | bytes 162248 | tf_op jit(solution)/shard_map/ppermute | solution.py:69
  363.7 57.3 %reduce-scatter.7.cloned.1.call-start = ((), (), s32[]{:S(2)}) async-start(), calls=%async_computation.19 | async-start | bytes 1474560 | tf_op jit(solution)/shard_map/reduce_scatter | solution.py:180
  363.7 6.1 %collective-permute-start.8 = (f32[13520]{0:T(1024)S(1)}, f32[13520]{0:T(1024)S(1)}, u32[]{:S(2)}, u32[]{:S(2)}) collective-permute-start(f32[13520]{0:T(1024)S(1)} %add.488), channel_id=1, source_target_pairs={{0,16},{8,24},{16,0},{24,8},{1,17},{9,25},{17,1},{25,9},{2,18},{10... | collective-permute-start | bytes 162248 | tf_op jit(solution)/shard_map/ppermute | solution.py:69
  390.9 10.8 %all-to-all-start.7 = ((bf16[4,72,144]{1,2,0:T(8,128)(2,1)}), bf16[4,72,144]{1,2,0:T(8,128)(2,1)S(1)}, u32[]{:S(2)}, u32[]{:S(2)}) async-start(bf16[4,72,144]{1,2,0:T(8,128)(2,1)} %copy.145), calls=%async_computation.8 | async-start | bytes 294912 | tf_op jit(solution)/shard_map/all_to_all | solution.py:58
  401.7 26.5 %all-to-all-start.5 = ((bf16[4,160,729]{2,1,0:T(8,128)(2,1)}), bf16[4,160,729]{2,1,0:T(8,128)(2,1)S(1)}, u32[]{:S(2)}, u32[]{:S(2)}) async-start(bf16[4,160,729]{2,1,0:T(8,128)(2,1)} %bitcast.35), calls=%async_computation.5 | async-start | bytes 1966080 | tf_op jit(solution)/shard_map/all_to_all | solution.py:46
  428.2 12.7 %all-to-all-start.6 = ((bf16[4,72,432]{2,1,0:T(8,128)(2,1)}), bf16[4,72,432]{2,1,0:T(8,128)(2,1)S(1)}, u32[]{:S(2)}, u32[]{:S(2)}) async-start(bf16[4,72,432]{2,1,0:T(8,128)(2,1)} %bitcast.176), calls=%async_computation.7 | async-start | bytes 589824 | tf_op jit(solution)/shard_map/all_to_all | solution.py:58
  (50 other events, 1091.3 us)
Sparse Core Ops, SparseCore 0:
  42.2 10.1 all-gather.7
  68.8 42.8 all-gather.5
  179.0 8.4 all-gather.9
  198.2 9.1 all-gather.11
  234.9 30.8 reduce-scatter.10
  268.9 30.3 reduce-scatter.8
  307.5 9.3 all-gather.13
  363.8 25.3 reduce-scatter.12
  392.4 28.5 reduce-scatter.6

commit v2 on v1

--- a/solution.py
+++ b/solution.py
@@ -38,6 +38,16 @@
 def gather_eight(block):
     rows = lax.all_gather(block, "row", axis=0, tiled=True)
     return lax.all_gather(rows, "col", axis=0, tiled=True)
+
+
+def send_copies(block, axis):
+    copies = jnp.broadcast_to(block, (lax.axis_size(axis),) + block.shape)
+    return lax.all_to_all(copies, axis, 0, 0).reshape(-1, block.shape[1])
+
+
+def zero_of(array):
+    first = lax.slice(array, (0,) * array.ndim, (1,) * array.ndim)
+    return first.reshape(()).astype(jnp.float32) * 0.0
 
 
 def sum_over_rows(half):
@@ -159,7 +169,9 @@
     feature = (
         ((place // width) % n_row) * n_col + place // (width * n_row)
     ) * width + place % width
-    order = (source == (feature % n_dp) * (D // n_dp) + feature // n_dp).astype(LOW)
+    order = lax.optimization_barrier(
+        (source == (feature % n_dp) * (D // n_dp) + feature // n_dp).astype(LOW)
+    )
 
     def mixed(vector):
         return vector.reshape(n_row, n_col, width).transpose(1, 0, 2).reshape(D)
@@ -167,25 +179,27 @@
     def plain(vector):
         return vector.reshape(n_col, n_row, width).transpose(1, 0, 2).reshape(D)
 
+    def dealt(vector):
+        return vector.reshape(D // n_dp, n_dp).T.reshape(D)
+
+    def undealt(vector):
+        return vector.reshape(n_dp, D // n_dp).T.reshape(D)
+
     def to_owner(rows, parts):
         return rows.reshape(shard_rows, parts, -1).transpose(1, 0, 2)
 
-    def gathered(blocks):
-        flat = blocks.reshape(n_row * shard_rows, blocks.shape[2])
-        return dot(order, lax.all_gather(flat, "dp", axis=0, tiled=True), 1, 0, LOW)
-
     def scattered(gradient):
         n = gradient.shape[1]
-        rows = dot(order, gradient.astype(LOW), 0, 0, LOW)
-        summed = lax.psum_scatter(rows, "dp", scatter_dimension=0, tiled=True)
-        blocks = exchange_rows(summed.reshape(n_row, shard_rows, n))
-        return blocks.astype(jnp.float32)
+        blocks = lax.all_to_all(gradient.reshape(n_dp, D // n_dp, n), "dp", 0, 0)
+        summed = jnp.sum(blocks.astype(jnp.float32), axis=0).astype(LOW)
+        return exchange_rows(summed.reshape(n_row, shard_rows, n)).astype(jnp.float32)
 
     def widened(blocks):
         return blocks.transpose(1, 0, 2).reshape(shard_rows, -1)
 
+    qkv_rows = exchange_rows(to_owner(qkv_master[:, 0].astype(LOW), n_row))
     x_all = gather_eight(inputs.T)
-    w_qkv = gathered(exchange_rows(to_owner(qkv_master[:, 0].astype(LOW), n_row)))
+    w_qkv = send_copies(qkv_rows.reshape(D // n_dp, -1), "dp")
     rest = jnp.concatenate(
         [
             to_owner(out_master[:, :, 0].T.astype(LOW), n_row),
@@ -194,19 +208,19 @@
         ],
         axis=2,
     )
-    w_rest = gathered(exchange_rows(rest))
-    w_out = w_rest[:, :width]
-    w_up = w_rest[:, width : width + hidden_width]
-    w_down = w_rest[:, width + hidden_width :]
-    cot_all = gather_eight(cotangent.T)
+    rest = exchange_rows(rest).reshape(D // n_dp, -1)
+    w_out = send_copies(rest[:, :width], "dp")
+    cot_rows = send_copies(cotangent.T, "row")
+    w_up = send_copies(rest[:, width : width + hidden_width], "dp")
+    w_down = send_copies(rest[:, width + hidden_width :], "dp")
 
     gain_one = mixed(norm_gains[0])
-    gain_two = mixed(norm_gains[1])
+    gain_two = dealt(norm_gains[1])
     shift_one = mixed(biases[:D])
-    shift_two = mixed(biases[D : 2 * D])
+    shift_two = dealt(biases[D : 2 * D])
     query_bias = lax.dynamic_slice_in_dim(biases, 2 * D + own * width, width).reshape(heads, HEAD)
     value_bias = lax.dynamic_slice_in_dim(biases, 3 * D + own * width, width).reshape(heads, HEAD)
-    out_bias = mixed(biases[4 * D : 5 * D])
+    out_bias = dealt(biases[4 * D : 5 * D])
     feature_start = (row * n_col + core) * width
     down_bias = lax.dynamic_slice_in_dim(biases, 5 * D + feature_start, width)
     up_bias = lax.dynamic_slice_in_dim(biases, 6 * D + own * hidden_width, hidden_width)
@@ -215,61 +229,65 @@
     )
 
     x_full = x_all.astype(jnp.float32)
-    center = x_full - jnp.sum(x_full, axis=0, keepdims=True) / D
+    x_mean = jnp.sum(x_full, axis=0, keepdims=True) / D
+    center = x_full - x_mean
     inverse_one = lax.rsqrt(jnp.sum(center * center, axis=0, keepdims=True) / D + NORM_EPS)
     za = (center * inverse_one * gain_one[:, None] + shift_one[:, None]).astype(LOW)
-
-    qkv = (dot(w_qkv, za, 0, 0) + qkv_bias).astype(LOW).reshape(heads, 3, HEAD, tokens)
-    queries, key_rows, values = qkv[:, 0], qkv[:, 1], qkv[:, 2]
-    attended, log_total = attend_forward(queries, key_rows, values)
-    attended = jnp.pad(attended.reshape(width, tokens), ((0, 0), (0, padded - tokens)))
-
-    half = padded // n_col
-    branch = reduce_eight(
-        lambda c: dot(lax.dynamic_slice_in_dim(attended, c * half, half, axis=1), w_out, 0, 1)
-    )
+    za = dot(order, za, 0, 0, LOW)
     token_start = own * chunk
     mine = (
         lax.broadcasted_iota(jnp.int32, (chunk, tokens), 1)
         == lax.broadcasted_iota(jnp.int32, (chunk, tokens), 0) + token_start
     ).astype(LOW)
-    middle = dot(mine, x_all, 1, 1) + branch + out_bias[None, :]
+    x_mine = dot(dot(mine, x_all, 1, 1, LOW), order, 1, 0)
+
+    qkv = (dot(w_qkv, za, 0, 0) + qkv_bias).astype(LOW).reshape(heads, 3, HEAD, tokens)
+    queries, key_rows, values = qkv[:, 0], qkv[:, 1], qkv[:, 2]
+    attended, log_total = attend_forward(queries, key_rows, values)
+    attended = jnp.pad(attended.reshape(width, tokens), ((0, 0), (0, padded - tokens)))
+
+    half = padded // n_col
+    branch = reduce_eight(
+        lambda c: dot(lax.dynamic_slice_in_dim(attended, c * half, half, axis=1), w_out, 0, 1)
+        + zero_of(cot_rows)
+    )
+
+    cot_all = lax.all_gather(cot_rows, "col", axis=0, tiled=True)
+    cot_all = jnp.pad(cot_all, ((0, 0), (0, padded - tokens)))
+    cot_dealt = dot(order, cot_all, 0, 0, LOW)
+    active_grad = dot(cot_dealt, w_down, 0, 0)
+    cot_mine = dot(mine, cot_dealt[:, :tokens], 1, 1)
+    qkv_mixed = dot(order, w_qkv, 1, 0, LOW)
+    down_mixed = dot(order, w_down, 1, 0, LOW)
+
+    middle = x_mine + branch + out_bias[None, :]
     center = middle - jnp.sum(middle, axis=1, keepdims=True) / D
     inverse_two = lax.rsqrt(jnp.sum(center * center, axis=1, keepdims=True) / D + NORM_EPS)
     normed_two = center * inverse_two
     zb = gather_eight((normed_two * gain_two + shift_two).astype(LOW))
 
     hidden = dot(zb, w_up, 1, 0) + up_bias
-    active_grad = dot(
-        jnp.pad(cot_all, ((0, 0), (0, padded - tokens))), w_down, 0, 0
-    )
     active, gelu_pullback = jax.vjp(lambda v: jax.nn.gelu(v, approximate=True), hidden)
     active = active.astype(LOW)
     hidden_grad = gelu_pullback(active_grad)[0].astype(LOW)
 
     two_grad = reduce_eight(lambda c: dot(take(hidden_grad, c, half), w_up, 1, 1))
-    cot_mine = dot(mine, cot_all, 1, 1)
+    down_blocks = scattered(dot(cot_dealt, active, 1, 0, LOW))
+    up_blocks = scattered(dot(zb, hidden_grad, 0, 0, LOW))
+
     scaled = two_grad * gain_two
     first_sum = jnp.sum(scaled, axis=1, keepdims=True) / D
     second_sum = jnp.sum(scaled * normed_two, axis=1, keepdims=True) / D
     middle_grad = cot_mine + inverse_two * (scaled - first_sum - normed_two * second_sum)
     branch_all = gather_eight(middle_grad.astype(LOW))
-    gain_two_grad = jnp.sum(two_grad * normed_two, axis=0)
-    shift_two_grad = jnp.sum(two_grad, axis=0)
-    out_bias_grad = jnp.sum(middle_grad.astype(LOW), axis=0, dtype=jnp.float32)
-    down_bias_grad = jnp.sum(cot_mine, axis=0)
-    up_bias_grad = jnp.sum(hidden_grad, axis=0, dtype=jnp.float32)
 
     attended_grad = dot(w_out, branch_all, 0, 1, LOW)[:, :tokens].reshape(heads, HEAD, tokens)
     qkv_grad = attend_backward(queries, key_rows, values, log_total, attended_grad)
-    bias_sums = jnp.sum(qkv_grad, axis=3, dtype=jnp.float32)
     qkv_grad = qkv_grad.reshape(3 * width, tokens)
     qkv_blocks = scattered(dot(za, qkv_grad, 1, 1, LOW))
 
-    one_part = dot(w_qkv, qkv_grad, 1, 0)
-    normed_one = (x_full - jnp.sum(x_full, axis=0, keepdims=True) / D) * inverse_one
-    gain_one_grad = jnp.sum(one_part * normed_one, axis=1)
-    shift_one_grad = jnp.sum(one_part, axis=1)
+    one_part = dot(qkv_mixed, qkv_grad, 1, 0)
+    normed_one = (x_full - x_mean) * inverse_one
     scaled_part = one_part * gain_one[:, None]
     sums = jnp.stack(
         [jnp.sum(scaled_part, axis=0), jnp.sum(scaled_part * normed_one, axis=0)], axis=0
@@ -283,18 +301,20 @@
         lambda c: lax.dynamic_index_in_dim(one_rows, c, 0, keepdims=False).astype(jnp.float32)
     )
     own_gain = lax.dynamic_slice_in_dim(norm_gains[0], feature_start, width)[:, None]
-    own_input = inputs.T.astype(jnp.float32)
-    own_normed = (own_input - jnp.sum(x_full, axis=0, keepdims=True) / D) * inverse_one
-    own_middle = lax.dynamic_slice_in_dim(branch_all, own * width, width, axis=1)[:tokens].T
-    input_grad = own_middle.astype(jnp.float32) + inverse_one * (
+    own_normed = (inputs.T.astype(jnp.float32) - x_mean) * inverse_one
+    own_order = lax.dynamic_slice_in_dim(order, own * width, width, axis=0)
+    own_middle = dot(own_order, branch_all, 1, 1)[:, :tokens]
+    input_grad = own_middle + inverse_one * (
         one_grad[:width] * own_gain
         - one_grad[width : width + 1] / D
         - own_normed * (one_grad[width + 1 : width + 2] / D)
     )
     input_grad = input_grad.astype(LOW).T
 
-    down_half = lambda c: dot(take(w_down, c, D // n_col), active, 1, 1)[:, :tokens] + dot(
-        lax.dynamic_slice_in_dim(middle, c * (D // n_col), D // n_col, axis=1),
+    later = zero_of(branch_all)
+    middle_mixed = dot(middle, order.astype(jnp.float32), 1, 1, precision=lax.Precision.HIGHEST)
+    down_half = lambda c: dot(take(down_mixed, c, D // n_col), active, 1, 1)[:, :tokens] + dot(
+        lax.dynamic_slice_in_dim(middle_mixed, c * (D // n_col), D // n_col, axis=1) + later,
         mine.astype(jnp.float32),
         0,
         0,
@@ -302,44 +322,50 @@
     )
     result = (reduce_eight(down_half) + down_bias[:, None]).astype(LOW).T
 
-    down_blocks = scattered(dot(jnp.pad(cot_all, ((0, 0), (0, padded - tokens))), active, 1, 0, LOW))
-    up_blocks = scattered(dot(zb, hidden_grad, 0, 0, LOW))
     out_blocks = scattered(dot(branch_all, attended, 0, 1, LOW))
 
-    gain_grad = jnp.stack([plain(gain_one_grad), plain(gain_two_grad)])
-    zeros = jnp.zeros(biases.shape, jnp.float32)
+    bias_sums = jnp.sum(qkv_grad, axis=1, dtype=jnp.float32).reshape(heads, 3, HEAD)
+    gain_one_grad = jnp.sum(one_part * normed_one, axis=1)
+    shift_one_grad = jnp.sum(one_part, axis=1)
+    gain_two_grad = jnp.sum(two_grad * normed_two, axis=0)
+    shift_two_grad = jnp.sum(two_grad, axis=0)
+    out_bias_grad = jnp.sum(middle_grad.astype(LOW), axis=0, dtype=jnp.float32)
+    down_bias_grad = jnp.sum(cot_mine, axis=0)
+    up_bias_grad = jnp.sum(hidden_grad, axis=0, dtype=jnp.float32)
     bias_grad = jnp.concatenate(
         [
+            plain(gain_one_grad),
+            undealt(gain_two_grad),
             plain(shift_one_grad),
-            plain(shift_two_grad),
+            undealt(shift_two_grad),
             jnp.zeros((2 * D,), jnp.float32),
-            plain(out_bias_grad),
-            plain(down_bias_grad),
+            undealt(out_bias_grad),
+            undealt(down_bias_grad),
             jnp.zeros((FF,), jnp.float32),
         ]
     )
-    bias_grad = lax.dynamic_update_slice_in_dim(
-        bias_grad, bias_sums[:, 0].reshape(width), 2 * D + own * width, 0
-    )
-    bias_grad = lax.dynamic_update_slice_in_dim(
-        bias_grad, bias_sums[:, 2].reshape(width), 3 * D + own * width, 0
-    )
-    bias_grad = lax.dynamic_update_slice_in_dim(
-        bias_grad, up_bias_grad, 6 * D + own * hidden_width, 0
-    )
-    total = all_sum(jnp.concatenate([gain_grad.reshape(-1), bias_grad]))
+    for piece, offset in (
+        (bias_sums[:, 0].reshape(width), 4 * D + own * width),
+        (bias_sums[:, 2].reshape(width), 5 * D + own * width),
+        (up_bias_grad, 8 * D + own * hidden_width),
+    ):
+        bias_grad = lax.dynamic_update_slice_in_dim(bias_grad, piece, offset, 0)
+    total = all_sum(bias_grad)
     gain_total = total[: 2 * D].reshape(2, D)
     bias_total = total[2 * D :]
 
+    later = zero_of(qkv_grad)
     q_new = adam_update(
         qkv_master, qkv_first, qkv_second, widened(qkv_blocks)[:, None], 0.03, 0.1
     )
     o_new = adam_update(
-        out_master, out_first, out_second, widened(out_blocks).T[:, :, None], 0.12, 0.1
-    )
-    u_new = adam_update(up_master, up_first, up_second, widened(up_blocks)[:, None], 0.03, 0.1)
+        out_master, out_first, out_second, widened(out_blocks + later).T[:, :, None], 0.12, 0.1
+    )
+    u_new = adam_update(
+        up_master, up_first, up_second, widened(up_blocks + later)[:, None], 0.03, 0.1
+    )
     d_new = adam_update(
-        down_master, down_first, down_second, widened(down_blocks).T[:, :, None], 0.02, 0.1
+        down_master, down_first, down_second, widened(down_blocks + later).T[:, :, None], 0.02, 0.1
     )
     g_new = adam_update(norm_gains, gain_first, gain_second, gain_total, 0.5, 0.0)
     b_new = adam_update(biases, bias_first, bias_second, bias_total, 0.5, 0.0)

time: 460 us -> 504 us (1.096)
  starting transfers between devices: 48.6 us -> 82.1 us
  local copies, waits for them, and re-layouts: 31.9 us -> 59.3 us
  waiting for transfers between devices: 127 us -> 113 us
  blocking collectives: 101 us -> 91.1 us
  other arithmetic: 39.1 us -> 44.9 us
    all_to_all x0 -> x8, starting transfers between devices: none -> 34.9 us  [the longest x4 17.9 us: send_copies(): return lax.all_to_all(copies, axis, 0, 0).reshape(-1, block.shape[1])]
    all_gather x1, waiting for transfers between devices: 28.6 us -> 0.01 us  [shards(): cot_all = lax.all_gather(cot_rows, 'col', axis=0, tiled=True)]
    all_to_all x0 -> x8, waiting for transfers between devices: none -> 26.5 us  [the longest x4 21.3 us: send_copies(): return lax.all_to_all(copies, axis, 0, 0).reshape(-1, block.shape[1])]
    unnamed x4 -> x0, matrix products: 25.4 us -> none
    dot_general x17 -> x24, matrix products: 55.9 us -> 76.8 us  [dot(): lax.dot_general(left, right, (((left_dim,), (right_dim,)), ((), ())), pre...]
    all_to_all x0 -> x1, blocking collectives: none -> 19.5 us  [send_copies(): return lax.all_to_all(copies, axis, 0, 0).reshape(-1, block.shape[1])]
    unnamed x10 -> x4, waiting for transfers between devices: 19.5 us -> 0.07 us
    all_to_all x4, waiting for transfers between devices: 53.2 us -> 70.5 us  [sum_over_rows(): lax.all_to_all(blocks, 'row', 0, 0).astype(jnp.float32)]
  transfers between devices with their start and end apart: 28 -> 31, of which waited for: 13 -> 16; matrix products, arithmetic and copies ran while one was open for 26% -> 33% of each run, Pallas kernels for 0% -> 0%
where the time goes in v2:
time: 504 us; the launch traced here: 496 us
  waiting for transfers between devices  113 us (22%)
  blocking collectives  91.1 us (18%)
  matrix products  87.6 us (17%)
  starting transfers between devices  82.1 us (16%)
  local copies, waits for them, and re-layouts  59.3 us (12%)
  other arithmetic  44.9 us (9%)
  between operations  17.5 us (3%)
    dot_general x24, matrix products, dot(): lax.dot_general(left, right, (((left_dim,), (right_dim,)), ((), ())), pre...  76.8 us
    all_gather x3, blocking collectives, gather_eight(): rows = lax.all_gather(block, 'row', axis=0, tiled=True)  71.6 us
    all_to_all x4, waiting for transfers between devices, sum_over_rows(): lax.all_to_all(blocks, 'row', 0, 0).astype(jnp.float32)  70.5 us
    all_to_all x6, starting transfers between devices, exchange_rows(): return lax.all_to_all(blocks, 'row', 0, 0)  26.6 us
    all_to_all x4, waiting for transfers between devices, send_copies(): return lax.all_to_all(copies, axis, 0, 0).reshape(-1, block.shape[1])  21.3 us
    all_to_all x1, blocking collectives, send_copies(): return lax.all_to_all(copies, axis, 0, 0).reshape(-1, block.shape[1])  19.5 us
    unnamed x139, local copies, waits for them, and re-layouts  19.3 us
    all_to_all x4, starting transfers between devices, send_copies(): return lax.all_to_all(copies, axis, 0, 0).reshape(-1, block.shape[1])  17.9 us
  transfers between devices with their start and end apart: 31, of which 16 were waited for; matrix products, arithmetic and copies ran while one was open for 33% of the time, Pallas kernels for 0%

profile of v2, /device:TPU:0, one launch (start us, length us, event | category | flops | bytes accessed | tf_op | source)
XLA Modules:
  0.0 495.6 jit_solution(14639479133965995515)
XLA Ops:
  10.9 6.3 %all-to-all-start.2 = ((bf16[4,72,432]{2,1,0:T(8,128)(2,1)}), bf16[4,72,432]{2,1,0:T(8,128)(2,1)S(1)}, u32[]{:S(2)}, u32[]{:S(2)}) async-start(bf16[4,72,432]{2,1,0:T(8,128)(2,1)} %copy.211), calls=%async_computation.2 | async-start | bytes 589824 | tf_op jit(solution)/shard_map/all_to_all | solution.py:68
  30.4 32.3 %all_gather.21 = bf16[576,729]{1,0:T(8,128)(2,1)} all-gather(bf16[144,729]{1,0:T(8,128)(2,1)S(1)} %bitcast.224), channel_id=1, replica_groups=mesh['dp'=4,'row'=4,'col'=2] {'row'}, dimensions={0}, use_global_device_ids=true | all-gather | bytes 1049760 | tf_op jit(solution)/shard_map/all_gather | solution.py:39
  63.7 5.1 %all-to-all-start.5 = ((bf16[4,144,729]{2,1,0:T(8,128)(2,1)}), bf16[4,144,729]{2,1,0:T(8,128)(2,1)S(1)}, u32[]{:S(2)}, u32[]{:S(2)}) async-start(bf16[4,144,729]{2,1,0:T(8,128)(2,1)} %broadcast_in_dim.19), calls=%async_computation.5 | async-start | bytes 1769472 | tf_op jit(solution)/shard_map/all_to_all | solution.py:45
  68.9 5.9 %fusion.12 = bf16[1152,1152]{1,0:T(8,128)(2,1)} fusion(s32[1152]{0:T(1024)S(1)} %get-tuple-element.181, s32[1152]{0:T(1024)S(1)} %get-tuple-element.182, s32[1152]{0:T(1024)S(1)} %get-tuple-element.179, s32[1152]{0:T(1024)S(1)} %get-tuple-element.185, s32[1152]{0:T(1024)S(1)} %get-tuple-element.180, s32[1152]{0:T(1024)S(1)} %get-tuple-element.186, ...), kind=kLoop, calls=%fused_computation.23 | loop fusion | flops 54411264 | bytes 2685312 | tf_op jit(solution)/shard_map/convert_element_type | solution.py:173
  75.8 11.2 %all-to-all-done.5 = bf16[4,144,729]{2,1,0:T(8,128)(2,1)S(1)} async-done(((bf16[4,144,729]{2,1,0:T(8,128)(2,1)}), bf16[4,144,729]{2,1,0:T(8,128)(2,1)S(1)}, u32[]{:S(2)}, u32[]{:S(2)}) %all-to-all-start.5) | async-done | bytes 839840 | tf_op jit(solution)/shard_map/all_to_all | solution.py:45
  93.3 4.4 all-to-all-done.4
  98.8 4.4 all-to-all-start.3
  106.4 5.7 %fusion.33 = bf16[1152,729]{0,1:T(8,128)(2,1)} fusion(bf16[1152,1152]{1,0:T(8,128)(2,1)} %fusion.12, bf16[1152,729]{1,0:T(8,128)(2,1)S(1)} %copy-done.1, f32[1152]{0:T(1024)S(1)} %add.395, f32[1152]{0:T(1024)S(1)} %mul.535, f32[729]{0:T(1024)S(1)} %add_rsqrt_fusion, f32[729]{0:T(1024)S(1)} %broadcast_multiply_fusion), kind=kOutput, calls=%fused_computation.63 | convolution fusion | flops 1939956480 | bytes 6028488 | tf_op jit(solution)/shard_map/dot_general | solution.py:20
  133.0 21.6 %all-to-all-done.6 = bf16[4,96,1152]{2,1,0:T(8,128)(2,1)} async-done(((bf16[4,96,1152]{2,1,0:T(8,128)(2,1)}), bf16[4,96,1152]{2,1,0:T(8,128)(2,1)}, u32[]{:S(2)}, u32[]{:S(2)}) %all-to-all-start.6) | async-done | bytes 884768 | tf_op jit(solution)/shard_map/all_to_all | solution.py:56
  159.3 19.5 %all_gather.23 = bf16[384,1152]{1,0:T(8,128)(2,1)} all-gather(bf16[96,1152]{1,0:T(8,128)(2,1)S(1)} %add_convert_fusion.6), channel_id=1, replica_groups=mesh['dp'=4,'row'=4,'col'=2] {'row'}, dimensions={0}, use_global_device_ids=true | all-gather | bytes 1105920 | tf_op jit(solution)/shard_map/all_gather | solution.py:39
  179.3 19.5 %all_to_all.95 = bf16[4,288,538]{2,1,0:T(8,128)(2,1)} all-to-all(bf16[4,288,538]{2,1,0:T(8,128)(2,1)S(1)} %broadcast_in_dim.20), channel_id=1, replica_groups=mesh['dp'=4,'row'=4,'col'=2] {'dp'}, dimensions={0} | all-to-all | bytes 2479104 | tf_op jit(solution)/shard_map/all_to_all | solution.py:45
  200.0 4.6 all-to-all-start.1
  204.7 6.2 %fusion.35 = bf16[1152,768]{0,1:T(8,128)(2,1)} fusion(bf16[1152,1152]{1,0:T(8,128)(2,1)} %fusion.12, bf16[1152,729]{1,0:T(8,128)(2,1)} %all-gather.9.cloned.1.call-done), kind=kOutput, calls=%fused_computation.68 | convolution fusion | flops 2038431744 | bytes 6103296 | tf_op jit(solution)/shard_map/dot_general | solution.py:20
  210.9 4.5 fusion.158
  219.2 6.4 %convert_reduce_fusion.6 = (f32[538]{0:T(1024)}, bf16[768,538]{0,1:T(8,128)(2,1)S(1)}, bf16[768,538]{0,1:T(8,128)(2,1)}) fusion(f32[768,538]{0,1:T(8,128)} %fusion.158, f32[538]{0:T(1024)S(1)} %dynamic_slice.54, bf16[1152,768]{0,1:T(8,128)(2,1)} %fusion.35, bf16[1152,538]{1,0:T(8,128)(2,1)} %bitcast.6), kind=kOutput, calls=%fused_computation.85 | convolution fusion | flops 962305024 | bytes 6318800 | tf_op jit(solution)/shard_map/dot_general | solution.py:20
  234.5 4.4 fusion.162
  238.9 18.4 %all-to-all-done.8 = bf16[4,96,1152]{2,1,0:T(8,128)(2,1)S(1)} async-done(((bf16[4,96,1152]{2,1,0:T(8,128)(2,1)}), bf16[4,96,1152]{2,1,0:T(8,128)(2,1)S(1)}, u32[]{:S(2)}, u32[]{:S(2)}) %all-to-all-start.8) | async-done | bytes 884768 | tf_op jit(solution)/shard_map/all_to_all | solution.py:56
  257.3 4.3 all-to-all-start.17
  263.7 19.9 %all_gather.26 = bf16[384,1152]{1,0:T(8,128)(2,1)} all-gather(bf16[96,1152]{1,0:T(8,128)(2,1)S(1)} %get-tuple-element.143), channel_id=1, replica_groups=mesh['dp'=4,'row'=4,'col'=2] {'row'}, dimensions={0}, use_global_device_ids=true | all-gather | bytes 1105920 | tf_op jit(solution)/shard_map/all_gather | solution.py:39
  288.0 4.3 fusion.161
  292.4 4.3 all-to-all-start.15
  296.8 5.3 %fusion.157 = bf16[1152,538]{0,1:T(8,128)(2,1)} fusion(bf16[1152,1152]{1,0:T(8,128)(2,1)} %fusion.12, bf16[1152,538]{1,0:T(8,128)(2,1)} %bitcast.6), kind=kOutput, calls=%fused_computation.260 | convolution fusion | flops 1427963904 | bytes 5133312 | tf_op jit(solution)/shard_map/dot_general | solution.py:20
  307.1 5.2 %all-to-all-done.15 = bf16[4,288,538]{2,1,0:T(8,128)(2,1)} async-done(((bf16[4,288,538]{2,1,0:T(8,128)(2,1)}), bf16[4,288,538]{2,1,0:T(8,128)(2,1)}, u32[]{:S(2)}, u32[]{:S(2)}) %all-to-all-start.15) | async-done | bytes 1239584 | tf_op jit(solution)/shard_map/all_to_all | solution.py:193
  342.4 5.3 %all-to-all-start.16 = ((bf16[4,72,538]{2,1,0:T(8,128)(2,1)}), bf16[4,72,538]{2,1,0:T(8,128)(2,1)S(1)}, u32[]{:S(2)}, u32[]{:S(2)}) async-start(bf16[4,72,538]{2,1,0:T(8,128)(2,1)} %bitcast.56), calls=%async_computation.16 | async-start | bytes 737280 | tf_op jit(solution)/shard_map/all_to_all | solution.py:68
  349.1 7.4 %fusion.151 = (f32[1152]{0:T(1024)S(1)}, bf16[1152,729]{0,1:T(8,128)(2,1)}, f32[1152,729]{0,1:T(8,128)}) fusion(bf16[432,729]{1,0:T(8,128)(2,1)} %bitcast.213, bf16[1152,1152]{1,0:T(8,128)(2,1)} %fusion.12, bf16[1152,432]{1,0:T(8,128)(2,1)} %bitcast.12), kind=kOutput, calls=%fused_computation.254 | convolution fusion | flops 1873890432 | bytes 9322848 | tf_op jit(solution)/shard_map/dot_general | solution.py:20
  364.4 5.1 %copy.226 = f32[1152,729]{1,0:T(8,128)} copy(f32[1152,729]{0,1:T(8,128)} %get-tuple-element.178) | data formatting | bytes 6718464 | tf_op jit(solution)/shard_map/dot_general | solution.py:20
  379.3 4.3 all-to-all-start.11
  409.4 4.4 all-to-all-start.12
  425.9 4.4 add_convert_fusion
  430.3 5.2 %all-to-all-start.9 = ((bf16[4,144,729]{2,1,0:T(8,128)(2,1)}), bf16[4,144,729]{2,1,0:T(8,128)(2,1)}, u32[]{:S(2)}, u32[]{:S(2)}) async-start(bf16[4,144,729]{2,1,0:T(8,128)(2,1)} %bitcast.30), calls=%async_computation.9 | async-start | bytes 1769472 | tf_op jit(solution)/shard_map/all_to_all | solution.py:56
  440.5 18.0 %all-to-all-done.9 = bf16[4,144,729]{2,1,0:T(8,128)(2,1)} async-done(((bf16[4,144,729]{2,1,0:T(8,128)(2,1)}), bf16[4,144,729]{2,1,0:T(8,128)(2,1)}, u32[]{:S(2)}, u32[]{:S(2)}) %all-to-all-start.9) | async-done | bytes 839840 | tf_op jit(solution)/shard_map/all_to_all | solution.py:56
  473.6 12.5 %all-to-all-done.10 = bf16[4,160,729]{2,1,0:T(8,128)(2,1)S(1)} async-done(((bf16[4,160,729]{2,1,0:T(8,128)(2,1)}), bf16[4,160,729]{2,1,0:T(8,128)(2,1)S(1)}, u32[]{:S(2)}, u32[]{:S(2)}) %all-to-all-start.10) | async-done | bytes 933152 | tf_op jit(solution)/shard_map/all_to_all | solution.py:56
  (357 shorter events, 188.0 us)
Async XLA Ops:
  10.9 15.9 %all-to-all-start.2 = ((bf16[4,72,432]{2,1,0:T(8,128)(2,1)}), bf16[4,72,432]{2,1,0:T(8,128)(2,1)S(1)}, u32[]{:S(2)}, u32[]{:S(2)}) async-start(bf16[4,72,432]{2,1,0:T(8,128)(2,1)} %copy.211), calls=%async_computation.2 | async-start | bytes 589824 | tf_op jit(solution)/shard_map/all_to_all | solution.py:68
  26.8 35.9 %all-to-all-start = ((bf16[4,72,1220]{2,1,0:T(8,128)(2,1)}), bf16[4,72,1220]{2,1,0:T(8,128)(2,1)S(1)}, u32[]{:S(2)}, u32[]{:S(2)}) async-start(bf16[4,72,1220]{2,1,0:T(8,128)(2,1)} %copy.208), calls=%async_computation | async-start | bytes 1474560 | tf_op jit(solution)/shard_map/all_to_all | solution.py:68
  30.3 73.4 %all-gather.5.cloned.1.call-start = ((), (), s32[]{:S(2)}) async-start(), calls=%async_computation.19 | async-start | bytes 2654208 | tf_op jit(solution)/shard_map/all_gather | solution.py:40
  63.7 23.2 %all-to-all-start.5 = ((bf16[4,144,729]{2,1,0:T(8,128)(2,1)}), bf16[4,144,729]{2,1,0:T(8,128)(2,1)S(1)}, u32[]{:S(2)}, u32[]{:S(2)}) async-start(bf16[4,144,729]{2,1,0:T(8,128)(2,1)} %broadcast_in_dim.19), calls=%async_computation.5 | async-start | bytes 1769472 | tf_op jit(solution)/shard_map/all_to_all | solution.py:45
  87.8 9.9 %all-to-all-start.4 = ((bf16[4,288,144]{1,2,0:T(8,128)(2,1)}), bf16[4,288,144]{1,2,0:T(8,128)(2,1)S(1)}, u32[]{:S(2)}, u32[]{:S(2)}) async-start(bf16[4,288,144]{1,2,0:T(8,128)(2,1)} %broadcast_in_dim.18), calls=%async_computation.4 | async-start | bytes 884736 | tf_op jit(solution)/shard_map/all_to_all | solution.py:45
  98.8 15.1 %all-to-all-start.3 = ((bf16[4,288,432]{2,1,0:T(8,128)(2,1)}), bf16[4,288,432]{2,1,0:T(8,128)(2,1)}, u32[]{:S(2)}, u32[]{:S(2)}) async-start(bf16[4,288,432]{2,1,0:T(8,128)(2,1)} %broadcast_in_dim.17), calls=%async_computation.3 | async-start | bytes 2359296 | tf_op jit(solution)/shard_map/all_to_all | solution.py:45
  122.2 2.8 collective-permute-start
  127.5 27.1 %all-to-all-start.6 = ((bf16[4,96,1152]{2,1,0:T(8,128)(2,1)}), bf16[4,96,1152]{2,1,0:T(8,128)(2,1)}, u32[]{:S(2)}, u32[]{:S(2)}) async-start(bf16[4,96,1152]{2,1,0:T(8,128)(2,1)} %bitcast.210), calls=%async_computation.6 | async-start | bytes 1769472 | tf_op jit(solution)/shard_map/all_to_all | solution.py:56
  131.8 72.9 %all-gather.9.cloned.1.call-start = ((), (), s32[]{:S(2)}) async-start(), calls=%async_computation.21 | async-start | bytes 2654208 | tf_op jit(solution)/shard_map/all_gather | solution.py:255
  132.9 201.1 %copy-start.49 = (s32[96]{0:T(128)}, s32[96]{0:T(128)S(1)}, u32[]{:S(2)}) copy-start(s32[96]{0:T(128)S(1)} %iota_add_fusion) | copy-start | bytes 1156
  132.9 78.0 %all-gather.7.cloned.1.call-start = ((), (), s32[]{:S(2)}) async-start(), calls=%async_computation.20 | async-start | bytes 2654208 | tf_op jit(solution)/shard_map/all_gather | solution.py:40
  200.0 19.2 %all-to-all-start.1 = ((bf16[4,288,538]{2,1,0:T(8,128)(2,1)}), bf16[4,288,538]{2,1,0:T(8,128)(2,1)}, u32[]{:S(2)}, u32[]{:S(2)}) async-start(bf16[4,288,538]{2,1,0:T(8,128)(2,1)} %broadcast_in_dim.16), calls=%async_computation.1 | async-start | bytes 2949120 | tf_op jit(solution)/shard_map/all_to_all | solution.py:45
  226.6 2.5 collective-permute-start.1
  231.0 26.3 %all-to-all-start.8 = ((bf16[4,96,1152]{2,1,0:T(8,128)(2,1)}), bf16[4,96,1152]{2,1,0:T(8,128)(2,1)S(1)}, u32[]{:S(2)}, u32[]{:S(2)}) async-start(bf16[4,96,1152]{2,1,0:T(8,128)(2,1)} %bitcast.211), calls=%async_computation.8 | async-start | bytes 1769472 | tf_op jit(solution)/shard_map/all_to_all | solution.py:56
  257.3 35.1 %all-to-all-start.17 = ((bf16[4,288,538]{2,1,0:T(8,128)(2,1)}), bf16[4,288,538]{2,1,0:T(8,128)(2,1)}, u32[]{:S(2)}, u32[]{:S(2)}) async-start(bf16[4,288,538]{2,1,0:T(8,128)(2,1)} %bitcast.196), calls=%async_computation.17 | async-start | bytes 2949120 | tf_op jit(solution)/shard_map/all_to_all | solution.py:193
  261.6 59.5 %all-gather.11.cloned.1.call-start = ((), (), s32[]{:S(2)}) async-start(), calls=%async_computation.22 | async-start | bytes 2654208 | tf_op jit(solution)/shard_map/all_gather | solution.py:40
  292.4 19.9 %all-to-all-start.15 = ((bf16[4,288,538]{2,1,0:T(8,128)(2,1)}), bf16[4,288,538]{2,1,0:T(8,128)(2,1)}, u32[]{:S(2)}, u32[]{:S(2)}) async-start(bf16[4,288,538]{2,1,0:T(8,128)(2,1)} %bitcast.200), calls=%async_computation.15 | async-start | bytes 2949120 | tf_op jit(solution)/shard_map/all_to_all | solution.py:193
  312.2 30.1 %all-to-all-start.18 = ((bf16[4,72,538]{2,1,0:T(8,128)(2,1)}), bf16[4,72,538]{2,1,0:T(8,128)(2,1)S(1)}, u32[]{:S(2)}, u32[]{:S(2)}) async-start(bf16[4,72,538]{2,1,0:T(8,128)(2,1)} %bitcast.59), calls=%async_computation.18 | async-start | bytes 737280 | tf_op jit(solution)/shard_map/all_to_all | solution.py:68
  339.5 86.4 %collective-permute-start.2 = (bf16[576,729]{1,0:T(8,128)(2,1)}, bf16[576,729]{1,0:T(8,128)(2,1)}, u32[]{:S(2)}, u32[]{:S(2)}) collective-permute-start(bf16[576,729]{1,0:T(8,128)(2,1)} %add_convert_fusion.1), channel_id=1, source_target_pairs={{0,1},{1,0},{2,3},{3,2},{4,5},{5,4},{6,7},{7,6},{8,9},{9,8},{10,11... | collective-permute-start | bytes 2519432 | tf_op jit(solution)/shard_map/ppermute | solution.py:35
  342.4 17.1 %all-to-all-start.16 = ((bf16[4,72,538]{2,1,0:T(8,128)(2,1)}), bf16[4,72,538]{2,1,0:T(8,128)(2,1)S(1)}, u32[]{:S(2)}, u32[]{:S(2)}) async-start(bf16[4,72,538]{2,1,0:T(8,128)(2,1)} %bitcast.56), calls=%async_computation.16 | async-start | bytes 737280 | tf_op jit(solution)/shard_map/all_to_all | solution.py:68
  359.5 19.8 %all-to-all-start.13 = ((bf16[4,288,144]{1,2,0:T(8,128)(2,1)}), bf16[4,288,144]{1,2,0:T(8,128)(2,1)}, u32[]{:S(2)}, u32[]{:S(2)}) async-start(bf16[4,288,144]{1,2,0:T(8,128)(2,1)} %copy.236), calls=%async_computation.13 | async-start | bytes 884736 | tf_op jit(solution)/shard_map/all_to_all | solution.py:193
  374.1 12.4 %collective-permute-start.4 = (f32[13520]{0:T(1024)S(1)}, f32[13520]{0:T(1024)S(1)}, u32[]{:S(2)}, u32[]{:S(2)}) collective-permute-start(f32[13520]{0:T(1024)S(1)} %dynamic_update_slice.11), channel_id=1, source_target_pairs={{0,1},{1,0},{2,3},{3,2},{4,5},{5,4},{6,7},{7,6},{8,9},{9,8},{10,11... | collective-permute-start | bytes 162248 | tf_op jit(solution)/shard_map/ppermute | solution.py:79
  379.3 20.8 %all-to-all-start.11 = ((bf16[4,288,432]{2,1,0:T(8,128)(2,1)}), bf16[4,288,432]{2,1,0:T(8,128)(2,1)S(1)}, u32[]{:S(2)}, u32[]{:S(2)}) async-start(bf16[4,288,432]{2,1,0:T(8,128)(2,1)} %fusion.160), calls=%async_computation.11 | async-start | bytes 2359296 | tf_op jit(solution)/shard_map/all_to_all | solution.py:193
  386.5 4.2 collective-permute-start.5
  390.7 5.4 %collective-permute-start.6 = (f32[13520]{0:T(1024)S(1)}, f32[13520]{0:T(1024)S(1)}, u32[]{:S(2)}, u32[]{:S(2)}) collective-permute-start(f32[13520]{0:T(1024)S(1)} %add.474), channel_id=1, source_target_pairs={{0,4},{2,6},{4,0},{6,2},{1,5},{3,7},{5,1},{7,3},{8,12},{10,14},{12... | collective-permute-start | bytes 162248 | tf_op jit(solution)/shard_map/ppermute | solution.py:79
  396.1 9.1 %collective-permute-start.7 = (f32[13520]{0:T(1024)S(1)}, f32[13520]{0:T(1024)}, u32[]{:S(2)}, u32[]{:S(2)}) collective-permute-start(f32[13520]{0:T(1024)S(1)} %add.475), channel_id=1, source_target_pairs={{0,8},{8,0},{16,24},{24,16},{1,9},{9,1},{17,25},{25,17},{2,10},{10... | collective-permute-start | bytes 162248 | tf_op jit(solution)/shard_map/ppermute | solution.py:79
  400.1 9.3 %all-to-all-start.14 = ((bf16[4,72,144]{1,2,0:T(8,128)(2,1)}), bf16[4,72,144]{1,2,0:T(8,128)(2,1)S(1)}, u32[]{:S(2)}, u32[]{:S(2)}) async-start(bf16[4,72,144]{1,2,0:T(8,128)(2,1)} %copy.237), calls=%async_computation.14 | async-start | bytes 294912 | tf_op jit(solution)/shard_map/all_to_all | solution.py:68
  406.0 19.0 %collective-permute-start.8 = (f32[13520]{0:T(1024)S(1)}, f32[13520]{0:T(1024)}, u32[]{:S(2)}, u32[]{:S(2)}) collective-permute-start(f32[13520]{0:T(1024)S(1)} %add.476), channel_id=1, source_target_pairs={{0,16},{8,24},{16,0},{24,8},{1,17},{9,25},{17,1},{25,9},{2,18},{10... | collective-permute-start | bytes 162248 | tf_op jit(solution)/shard_map/ppermute | solution.py:79
  409.4 20.9 %all-to-all-start.12 = ((bf16[4,72,432]{2,1,0:T(8,128)(2,1)}), bf16[4,72,432]{2,1,0:T(8,128)(2,1)S(1)}, u32[]{:S(2)}, u32[]{:S(2)}) async-start(bf16[4,72,432]{2,1,0:T(8,128)(2,1)} %bitcast.46), calls=%async_computation.12 | async-start | bytes 589824 | tf_op jit(solution)/shard_map/all_to_all | solution.py:68
  425.0 12.7 %collective-permute-start.3 = (bf16[640,729]{0,1:T(8,128)(2,1)}, bf16[640,729]{0,1:T(8,128)(2,1)}, u32[]{:S(2)}, u32[]{:S(2)}) collective-permute-start(bf16[640,729]{0,1:T(8,128)(2,1)} %bitcast.207), channel_id=1, source_target_pairs={{0,1},{1,0},{2,3},{3,2},{4,5},{5,4},{6,7},{7,6},{8,9},{9,8},{10,11... | collective-permute-start | bytes 2799368 | tf_op jit(solution)/shard_map/ppermute | solution.py:35
  430.3 28.2 %all-to-all-start.9 = ((bf16[4,144,729]{2,1,0:T(8,128)(2,1)}), bf16[4,144,729]{2,1,0:T(8,128)(2,1)}, u32[]{:S(2)}, u32[]{:S(2)}) async-start(bf16[4,144,729]{2,1,0:T(8,128)(2,1)} %bitcast.30), calls=%async_computation.9 | async-start | bytes 1769472 | tf_op jit(solution)/shard_map/all_to_all | solution.py:56
  458.5 27.6 %all-to-all-start.10 = ((bf16[4,160,729]{2,1,0:T(8,128)(2,1)}), bf16[4,160,729]{2,1,0:T(8,128)(2,1)S(1)}, u32[]{:S(2)}, u32[]{:S(2)}) async-start(bf16[4,160,729]{2,1,0:T(8,128)(2,1)} %bitcast.41), calls=%async_computation.10 | async-start | bytes 1966080 | tf_op jit(solution)/shard_map/all_to_all | solution.py:56
  (58 other events, 447.2 us)
Sparse Core Ops, SparseCore 0:
  62.8 11.6 all-gather.4
  134.2 10.5 all-gather.8
  179.0 8.5 all-gather.6
  283.7 9.6 all-gather.10
